TPU v7x, 32 devices: a whole 2x2x4 slice. The times are simulated.
32 devices in a mesh: seq: 4 (over y, x), tp: 8 (over z, core).
Axes of the slice: x: 2, y: 2, z: 4, core: 2. Of those that a mesh axis runs over, the one named last changes fastest.
Arguments:
- hidden_in: bfloat16 [24, 4, 1024], P('tp'), may hold values from -6 to 6
- new_query: bfloat16 [24, 4, 1024], P('tp'), may hold values from -70 to 70
- new_key: bfloat16 [24, 4, 1024], P('tp'), may hold values from -15 to 15
- new_value: bfloat16 [24, 4, 1024], P('tp'), may hold values from -6 to 6
- key_cache: bfloat16 [24, 4096, 1024], P('tp', 'seq'), may hold values from -16 to 16
- value_cache: bfloat16 [24, 4096, 1024], P('tp', 'seq'), may hold values from -6 to 6
- lengths: int32 [24], P('tp'), may hold values from 64 to 4096, as said below
- out_weight: bfloat16 [1024, 1024], replicated, may hold values from -0.1875 to 0.1875
- norm_gain: float32 [1024], replicated, may hold values from 0.5 to 1.5
- router_weight: bfloat16 [1024, 16], replicated, may hold values from -0.1875 to 0.1875
- expert_ids: int32 [24, 4, 2], P('tp'), may hold values from 0 to 15, all different within a row
- gate_weight: bfloat16 [45056, 1024], P(('seq', 'tp')), may hold values from -0.1875 to 0.1875
- up_weight: bfloat16 [45056, 1024], P(('seq', 'tp')), may hold values from -0.1875 to 0.1875
- down_weight: bfloat16 [45056, 1024], P(('seq', 'tp')), may hold values from -0.109375 to 0.109375
Outputs:
- attn_out: bfloat16 [24, 4, 1024], P('tp', None, 'seq')
- layer_out: bfloat16 [24, 4, 1024], P('tp', None, 'seq')
Inputs may be any that keep to these rules, and one draw needn't show every extreme that they name: `lengths`: each length is 4096 or between 64 and 128; some request has 4096.
All inputs are finite; a program needn't handle non-finite values.
Results may differ from a plain program's by a relative error of at most 0.014.
Values may be sent and summed in bfloat16 or wider, within the bound.
No kernel may reach another device: no remote copies, remote signals or barrier semaphores. Data moves between devices by JAX's collectives and lax.ppermute only.
A program may use at most 64 MiB of HBM per device.

v0:
```python
import jax
import jax.numpy as jnp
from jax import lax
from jax.sharding import PartitionSpec as P

HEADS = 16


masked_score = -1e30
norm_epsilon = 1e-06


def entering(part, axis, combine, identity):
    place = lax.axis_index(axis)
    gathered = lax.all_gather(part, axis)
    state = jnp.zeros_like(part) + jnp.asarray(identity, part.dtype)

    def one(turn, state):
        return combine(state, lax.dynamic_index_in_dim(gathered, turn, 0, False))

    return lax.fori_loop(0, place, one, state)


def add_counts(former, latter):
    return former + latter


def pick_slot(chosen_ids, earlier):
    onehot = chosen_ids[..., None] == jnp.arange(earlier.shape[2], dtype=jnp.int32)
    return jnp.sum(jnp.where(onehot, earlier[:, :, None, :], 0), axis=3)


def body(
    hidden_in,
    new_query,
    new_key,
    new_value,
    key_cache,
    value_cache,
    lengths,
    out_weight,
    norm_gain,
    router_weight,
    expert_ids,
    gate_weight,
    up_weight,
    down_weight,
):
    req_dev, steps, width = hidden_in.shape
    block = key_cache.shape[1]
    head_size = width // HEADS
    scale = head_size ** (-0.5)
    seq_index = lax.axis_index("seq")
    tp_index = lax.axis_index("tp")
    seq_size = lax.axis_size("seq")
    tp_size = lax.axis_size("tp")
    queries = new_query.reshape(req_dev, steps, HEADS, head_size)
    cache_keys = key_cache.reshape(req_dev, block, HEADS, head_size)
    cache_values = value_cache.reshape(req_dev, block, HEADS, head_size)
    fresh_keys = new_key.reshape(req_dev, steps, HEADS, head_size)
    fresh_values = new_value.reshape(req_dev, steps, HEADS, head_size)
    scores = (
        jnp.einsum("rthe,rphe->rhtp", queries, cache_keys, preferred_element_type=jnp.float32)
        * scale
    )
    positions = seq_index * block + jnp.arange(block, dtype=jnp.int32)
    usable = (positions[None, :] < lengths[:, None])[:, None, None, :]
    scores = jnp.where(usable, scores, masked_score)
    fresh_scores = (
        jnp.einsum("rthe,rshe->rhts", queries, fresh_keys, preferred_element_type=jnp.float32)
        * scale
    )
    causal = (jnp.arange(steps)[:, None] >= jnp.arange(steps)[None, :]) & (seq_index == 0)
    fresh_scores = jnp.where(causal, fresh_scores, masked_score)
    local_max = jnp.maximum(jnp.max(scores, axis=3), jnp.max(fresh_scores, axis=3))
    weights = jnp.where(usable, jnp.exp(scores - local_max[..., None]), 0.0)
    fresh_weights = jnp.where(causal, jnp.exp(fresh_scores - local_max[..., None]), 0.0)
    totals = jnp.sum(weights, axis=3) + jnp.sum(fresh_weights, axis=3)
    gathered_values = jnp.einsum(
        "rhtp,rphe->rhte",
        weights.astype(jnp.bfloat16),
        cache_values,
        preferred_element_type=jnp.float32,
    )
    gathered_values = gathered_values + jnp.einsum(
        "rhts,rshe->rhte",
        fresh_weights.astype(jnp.bfloat16),
        fresh_values,
        preferred_element_type=jnp.float32,
    )
    overall = lax.pmax(local_max, "seq")
    factors = jnp.exp(local_max - overall)
    totals, gathered_values = (
        lax.psum((totals * factors).astype(jnp.bfloat16), "seq").astype(jnp.float32),
        lax.psum((gathered_values * factors[..., None]).astype(jnp.bfloat16), "seq").astype(
            jnp.float32
        ),
    )
    context = (
        (gathered_values / totals[..., None])
        .transpose(0, 2, 1, 3)
        .reshape(req_dev, steps, width)
        .astype(jnp.bfloat16)
    )
    attention = jnp.einsum("rtd,de->rte", context, out_weight, preferred_element_type=jnp.float32)
    feature_block = width // seq_size
    attn_out = lax.dynamic_slice_in_dim(
        attention, seq_index * feature_block, feature_block, 2
    ).astype(jnp.bfloat16)
    residual = hidden_in.astype(jnp.float32) + attention
    normed = (
        residual
        * lax.rsqrt(jnp.mean(residual * residual, axis=-1, keepdims=True) + norm_epsilon)
        * norm_gain
    ).astype(jnp.bfloat16)
    experts = router_weight.shape[1]
    topk = expert_ids.shape[2]
    requests = req_dev * tp_size
    capacity = (5 * requests * topk + 4 * experts - 1) // (4 * experts)
    expert_range = jnp.arange(experts, dtype=jnp.int32)
    local_hits = jnp.sum((expert_ids[..., None] == expert_range).astype(jnp.int32), axis=2)
    counts = jnp.sum(local_hits, axis=0)
    before = entering(counts, "tp", add_counts, jnp.zeros_like(counts))
    earlier = (before[None] + jnp.cumsum(local_hits, axis=0) - local_hits).astype(jnp.int32)
    routing = jnp.concatenate([expert_ids, pick_slot(expert_ids, earlier)], axis=2)
    all_routing = lax.all_gather(routing, "tp", axis=0, tiled=True)
    all_ids = all_routing[:, :, :topk]
    all_slots = all_routing[:, :, topk:]
    all_normed = lax.all_gather(normed, "tp", axis=0, tiled=True)
    logits = jnp.einsum(
        "rtd,de->rte", all_normed, router_weight, preferred_element_type=jnp.float32
    )
    onehot = all_ids[..., None] == expert_range
    chosen = jnp.sum(jnp.where(onehot, logits[:, :, None, :], 0.0), axis=3)
    share = 1.0 / (1.0 + jnp.exp(chosen[:, :, ::-1] - chosen))
    slices = seq_size * tp_size // experts
    mine = (seq_index * tp_size + tp_index) // slices
    match = all_ids == mine
    slot_mine = jnp.sum(jnp.where(match, all_slots, 0), axis=2)
    share_mine = jnp.sum(jnp.where(match, share, 0.0), axis=2)
    kept = jnp.any(match, axis=2) & (slot_mine < capacity)
    select = kept[None] & (slot_mine[None] == jnp.arange(capacity, dtype=jnp.int32)[:, None, None])
    buffer = (
        jnp.einsum(
            "crt,rtd->tcd",
            select.astype(jnp.bfloat16),
            all_normed,
            preferred_element_type=jnp.float32,
        )
        .astype(jnp.bfloat16)
        .reshape(steps * capacity, width)
    )
    contract = (((1,), (1,)), ((), ()))
    gate = lax.dot_general(buffer, gate_weight, contract, preferred_element_type=jnp.float32)
    upward = lax.dot_general(buffer, up_weight, contract, preferred_element_type=jnp.float32)
    inner = (jax.nn.gelu(gate) * upward).astype(jnp.bfloat16)
    produced = jnp.dot(inner, down_weight, preferred_element_type=jnp.float32)
    placed = select.astype(jnp.float32) * share_mine[None]
    term = jnp.einsum(
        "crt,tcd->rtd",
        placed,
        produced.reshape(steps, capacity, width),
        precision=lax.Precision.HIGHEST,
    )
    row_sums = lax.psum_scatter(term.astype(jnp.bfloat16), "tp", scatter_dimension=0, tiled=True)
    mixture = lax.psum_scatter(row_sums, "seq", scatter_dimension=2, tiled=True).astype(jnp.float32)
    own_residual = lax.dynamic_slice_in_dim(residual, seq_index * feature_block, feature_block, 2)
    layer_out = (own_residual + mixture).astype(jnp.bfloat16)
    return (attn_out, layer_out)


def solution(mesh):
    return jax.shard_map(
        body,
        mesh=mesh,
        in_specs=(
            P("tp", None, None),
            P("tp", None, None),
            P("tp", None, None),
            P("tp", None, None),
            P("tp", "seq", None),
            P("tp", "seq", None),
            P("tp"),
            P(),
            P(),
            P(),
            P("tp", None, None),
            P(("seq", "tp"), None),
            P(("seq", "tp"), None),
            P(("seq", "tp"), None),
        ),
        out_specs=(P("tp", None, "seq"), P("tp", None, "seq")),
        check_vma=False,
    )
```

profile of v0, /device:TPU:1, one launch (start us, length us, event | category | flops | bytes accessed | tf_op | source)
XLA Modules:
  0.0 212.1 jit_solution(17920888552861891735)
XLA Ops:
  7.2 1.0 reshape.92
  8.3 8.7 %copy.129 = bf16[3,1024,1024]{1,2,0:T(8,128)(2,1)} copy(bf16[3,1024,1024]{2,1,0:T(8,128)(2,1)} %param.20) | data formatting | bytes 12582912 | tf_op args[4]
  17.0 0.2 fusion.30
  17.6 4.6 %fusion.61 = (f32[3,16,4]{2,1,0:T(8,128)S(1)}, f32[3,16,4,1024]{3,2,1,0:T(4,128)}) fusion(bf16[3,1024,16,64]{1,3,2,0:T(8,128)(2,1)} %bitcast.35, bf16[3,4,16,64]{3,2,1,0:T(8,128)(2,1)S(1)} %reshape.92, pred[3,1024]{1,0:T(4,128)(4,1)S(1)} %broadcast_compare_fusion), kind=kOutput, calls=%fused_computation.93 | convolution fusion | flops 25755456 | bytes 7106304 | tf_op jit(solution)/shard_map/rthe,rphe->rhtp/dot_general | solution.py:63
  22.4 13.3 %pmax.7 = f32[3,16,4]{2,1,0:T(8,128)S(1)} all-reduce(f32[3,16,4]{2,1,0:T(8,128)S(1)} %max.9), channel_id=1, replica_groups=mesh['seq'=4,'tp'=8] {'seq'}, use_global_device_ids=true, to_apply=%region_2.3 | all-reduce | flops 192 | bytes 1536 | tf_op jit(solution)/shard_map/pmax | solution.py:91
  35.7 1.6 fusion.9
  37.5 8.6 %copy.135 = bf16[3,1024,1024]{1,2,0:T(8,128)(2,1)} copy(bf16[3,1024,1024]{2,1,0:T(8,128)(2,1)} %param.21) | data formatting | bytes 12582912 | tf_op args[5]
  46.1 4.8 %fusion.11 = f32[3,16,4,64]{3,2,1,0:T(4,128)S(1)} fusion(bf16[3,1024,16,64]{1,3,2,0:T(8,128)(2,1)} %bitcast.36, f32[3,16,4,1024]{3,2,1,0:T(4,128)} %get-tuple-element.49, f32[3,16,4]{2,1,0:T(8,128)S(1)} %max.9, pred[3,1024]{1,0:T(4,128)(4,1)S(1)} %broadcast_compare_fusion), kind=kOutput, calls=%fused_computation.19 | convolution fusion | flops 25755648 | bytes 7130880 | tf_op jit(solution)/shard_map/rhtp,rphe->rhte/dot_general | solution.py:79
  51.0 0.2 copy.137
  51.3 0.2 fusion.6
  51.5 11.8 %all-reduce.1 = (bf16[3,16,4,64]{3,2,1,0:T(4,128)(2,1)S(1)}, bf16[3,16,4]{2,1,0:T(8,128)(2,1)S(1)}) all-reduce(bf16[3,16,4,64]{3,2,1,0:T(4,128)(2,1)S(1)} %fusion.6, bf16[3,16,4]{2,1,0:T(8,128)(2,1)S(1)} %get-tuple-element.42), channel_id=1, replica_groups=mesh['seq'=4,'tp'=8] {'seq'}, use_global_device_ids=true, to_apply=%region_3.4 | all-reduce | flops 12480 | bytes 49920 | tf_op jit(solution)/shard_map/psum | solution.py:95
  63.6 2.1 multiply_reduce_fusion
  65.7 22.0 %all_gather.15 = bf16[24,4,1024]{2,1,0:T(4,128)(2,1)S(1)} all-gather(bf16[3,4,1024]{2,1,0:T(4,128)(2,1)S(1)} %multiply_convert_fusion), channel_id=1, replica_groups=mesh['seq'=4,'tp'=8] {'tp'}, dimensions={0}, use_global_device_ids=true | all-gather | bytes 221184 | tf_op jit(solution)/shard_map/all_gather | solution.py:129
  87.9 12.7 %all-gather.1 = s32[8,4,16]{2,1,0:T(4,128)S(1)} all-gather(s32[1,4,16]{2,1,0:T(4,128)S(1)} %bitcast.39), channel_id=2, replica_groups=mesh['seq'=4,'tp'=8] {'tp'}, dimensions={0}, use_global_device_ids=true | all-gather | bytes 2304 | tf_op jit(solution)/shard_map/all_gather | solution.py:15
  100.6 0.3 select_reduce_fusion.1
  101.0 14.0 %all_gather.14 = s32[24,4,4]{2,1,0:T(4,128)S(1)} all-gather(s32[3,4,4]{2,1,0:T(4,128)S(1)} %copy.141), channel_id=1, replica_groups=mesh['seq'=4,'tp'=8] {'tp'}, dimensions={0}, use_global_device_ids=true | all-gather | bytes 1728 | tf_op jit(solution)/shard_map/all_gather | solution.py:126
  115.1 0.3 fusion.16
  116.0 0.2 convolution_convert_fusion.1
  116.2 0.9 fusion.62
  117.1 3.9 %fusion.7 = f32[16,1024]{1,0:T(8,128)S(1)} fusion(bf16[1408,1024]{1,0:T(8,128)(2,1)} %param.29, bf16[16,1024]{1,0:T(8,128)(2,1)S(1)} %reshape.97, bf16[1408,1024]{1,0:T(8,128)(2,1)} %param.28, f32[16,1408]{1,0:T(8,128)S(1)} %fusion.62), kind=kOutput, calls=%fused_computation.13 | convolution fusion | flops 92499968 | bytes 5955584 | tf_op jit(solution)/shard_map/dot_general | solution.py:157
  121.1 0.5 fusion.4
  121.6 0.8 copy.152
  122.5 0.6 dynamic-slice
  123.8 50.1 %all-reduce.4.cloned.1.call-done = bf16[24,4,1024]{2,1,0:T(4,128)(2,1)} async-done(((bf16[24,4,1024]{2,1,0:T(4,128)(2,1)}), bf16[24,4,1024]{2,1,0:T(4,128)(2,1)}) %all-reduce.4.cloned.1.call-update) | async-done | bytes 196624
  173.9 0.7 constant_dynamic-slice_fusion
  174.6 1.4 copy.153
  176.1 3.0 %reshape.105 = bf16[1024,12]{1,0:T(8,128)(2,1)} reshape(bf16[1024,3,4]{2,1,0:T(4,128)(2,1)} %bitcast.37) | data formatting | bytes 49152
  179.1 0.6 dynamic-slice_convert_fusion
  179.7 23.8 %reduce-scatter.4.cloned.1.call-done = bf16[256,12]{1,0:T(8,128)(2,1)} async-done(((bf16[1024,12]{1,0:T(8,128)(2,1)}), bf16[256,12]{1,0:T(8,128)(2,1)}) %reduce-scatter.4.cloned.1.call-update) | async-done | bytes 6160
  203.5 1.0 reshape.106
  204.5 0.2 copy.154
  204.6 0.6 add_convert_fusion
  (62 shorter events, 2.5 us)
Async XLA Ops:
  7.2 109.1 %copy-start = (bf16[1408,1024]{1,0:T(8,128)(2,1)S(1)}, bf16[1408,1024]{1,0:T(8,128)(2,1)}, u32[]{:S(2)}) copy-start(bf16[1408,1024]{1,0:T(8,128)(2,1)} %param.27) | copy-start | bytes 8650756
  7.2 166.7 %all-reduce.4.cloned.1.call-start = ((), (), s32[]{:S(2)}) async-start(), calls=%async_computation.2 | async-start | bytes 393216
  8.2 8.7 %copy-start.3 = (bf16[3,4,1024]{2,1,0:T(4,128)(2,1)S(1)}, bf16[3,4,1024]{2,1,0:T(4,128)(2,1)}, u32[]{:S(2)}) copy-start(bf16[3,4,1024]{2,1,0:T(4,128)(2,1)} %param.18) | copy-start | bytes 73732
  8.2 9.3 %copy-start.6 = (s32[3]{0:T(128)S(1)}, s32[3]{0:T(128)}, u32[]{:S(2)}) copy-start(s32[3]{0:T(128)} %param.22) | copy-start | bytes 40
  46.1 5.0 %copy-start.4 = (bf16[3,4,1024]{2,1,0:T(4,128)(2,1)S(1)}, bf16[3,4,1024]{2,1,0:T(4,128)(2,1)}, u32[]{:S(2)}) copy-start(bf16[3,4,1024]{2,1,0:T(4,128)(2,1)} %param.19) | copy-start | bytes 73732
  46.1 17.4 %copy-start.2 = (bf16[3,4,1024]{2,1,0:T(4,128)(2,1)S(1)}, bf16[3,4,1024]{2,1,0:T(4,128)(2,1)}, u32[]{:S(2)}) copy-start(bf16[3,4,1024]{2,1,0:T(4,128)(2,1)} %param.16) | copy-start | bytes 73732
  51.0 14.7 %copy-start.5 = (f32[1024]{0:T(1024)S(1)}, f32[1024]{0:T(1024)}, u32[]{:S(2)}) copy-start(f32[1024]{0:T(1024)} %param.24) | copy-start | bytes 12292
  51.0 36.8 %copy-start.1 = (s32[3,4,2]{1,2,0:T(2,128)S(1)}, s32[3,4,2]{1,2,0:T(2,128)}, u32[]{:S(2)}) copy-start(s32[3,4,2]{1,2,0:T(2,128)} %param.26) | copy-start | bytes 292
  51.0 64.1 %copy-start.7 = (bf16[1024,16]{0,1:T(8,128)(2,1)S(1)}, bf16[1024,16]{0,1:T(8,128)(2,1)}, u32[]{:S(2)}) copy-start(bf16[1024,16]{0,1:T(8,128)(2,1)} %param.25) | copy-start | bytes 98308
  117.1 5.4 %copy-start.8 = (u32[32]{0:T(128)S(1)}, u32[32]{0:T(128)}, u32[]{:S(2)}) copy-start(u32[32]{0:T(128)} %constant.79) | copy-start | bytes 388
  122.5 81.1 %reduce-scatter.4.cloned.1.call-start = ((), (), s32[]{:S(2)}) async-start(), calls=%async_computation.1 | async-start | bytes 327680
Sparse Core Ops, SparseCore 0:
  122.6 51.2 all-reduce.3
  179.2 24.2 reduce-scatter.3
where the time goes:
time: 214 us; the launch traced here: 212 us
  waiting for transfers between devices  74 us (35%)
  blocking collectives  73.8 us (34%)
  local copies, waits for them, and re-layouts  28.3 us (13%)
  matrix products  17.7 us (8%)
  between operations  14.9 us (7%)
  other arithmetic  3.28 us (2%)
    unnamed x4, waiting for transfers between devices  74 us
    unnamed x30, local copies, waits for them, and re-layouts  24.6 us
    all_gather x1, blocking collectives, body(): all_normed = lax.all_gather(normed, 'tp', axis=0, tiled=True)  22 us
    all_gather x1, blocking collectives, body(): all_routing = lax.all_gather(routing, 'tp', axis=0, tiled=True)  14 us
    pmax x1, blocking collectives, body(): overall = lax.pmax(local_max, 'seq')  13.3 us
    all_gather x1, blocking collectives, entering(): gathered = lax.all_gather(part, axis)  12.7 us
    psum x1, blocking collectives, body(): lax.psum((gathered_values * factors[..., None]).astype(jnp.bfloat16), 'seq')  11.8 us
    dot_general x1, matrix products, body(): jnp.einsum('rhtp,rphe->rhte', weights.astype(jnp.bfloat16), cache_values,...  4.84 us
  transfers between devices with their start and end apart: 2, of which 2 were waited for; matrix products, arithmetic and copies ran while one was open for 1% of the time, Pallas kernels for 0%

commit v1 on v0

v1 whole, which is shorter than its diff:
```python
import functools

import jax
import jax.numpy as jnp
from jax import lax
from jax.experimental import pallas as pl
from jax.experimental.pallas import tpu as pltpu
from jax.sharding import PartitionSpec as P

HEADS = 16
SHORT = 128
ROWS = 16
LANES = 128
masked_score = -1e30
norm_epsilon = 1e-06
NT = (((1,), (1,)), ((), ()))
TN = (((0,), (0,)), ((), ()))


def iota(shape, dim):
    return lax.broadcasted_iota(jnp.int32, shape, dim)


def three_parts(x):
    hi = x.astype(jnp.bfloat16).astype(jnp.float32)
    mid = (x - hi).astype(jnp.bfloat16).astype(jnp.float32)
    return hi, mid, x - hi - mid


def tiled(x, times):
    return jnp.concatenate([x] * times, axis=0)


def attend(lens, q_ref, nk_ref, nv_ref, k_hbm, v_hbm, out_ref, kbuf, vbuf, acc, meta, sems):
    requests, block, width = k_hbm.shape
    steps = q_ref.shape[1]
    head = width // HEADS
    scale = head ** (-0.5)
    group = 256 // head
    chunks = width // 256
    rows = group * steps
    seq = lax.axis_index("seq")

    def moves(r, count):
        pair = []
        for which, (src, dst) in enumerate(((k_hbm, kbuf), (v_hbm, vbuf))):
            pair.append(
                pltpu.make_async_copy(
                    src.at[r, pl.ds(0, count)], dst.at[r, pl.ds(0, count)], sems.at[which, r]
                )
            )
        return pair

    left = [lens[r] - seq * block for r in range(requests)]
    for r in range(requests):

        @pl.when(left[r] >= block)
        def _():
            for move in moves(r, block):
                move.start()

        @pl.when((left[r] > 0) & (left[r] < block))
        def _():
            for move in moves(r, SHORT):
                move.start()

    acc[...] = jnp.zeros_like(acc)
    meta[...] = jnp.where(iota(meta.shape, 1) // HEADS == 3, 1.0, 0.0)

    diag = iota((rows, 256), 0) // steps == iota((rows, 256), 1) // head
    diag_all = iota((rows, width), 0) // steps == (iota((rows, width), 1) % 256) // head
    all_rows = chunks * rows

    def one(r, count, whole):
        key_move, value_move = moves(r, count)
        tiled_q = tiled(q_ref[r].astype(jnp.float32), group)
        query = jnp.where(diag_all, tiled_q, 0.0).astype(jnp.bfloat16)
        fresh_k = tiled(nk_ref[r].astype(jnp.float32), group).astype(jnp.bfloat16)
        fresh_v = tiled(nv_ref[r].astype(jnp.float32), group).astype(jnp.bfloat16)
        fresh = jnp.concatenate(
            [
                lax.dot_general(
                    query[:, c * 256 : (c + 1) * 256],
                    fresh_k[:, c * 256 : (c + 1) * 256],
                    NT,
                    preferred_element_type=jnp.float32,
                )
                for c in range(chunks)
            ],
            axis=0,
        )
        row = iota(fresh.shape, 0)
        column = iota(fresh.shape, 1)
        allowed = (column < steps) & (column <= row % steps) & (seq == 0)
        fresh = jnp.where(allowed, fresh * scale, masked_score)
        key_move.wait()
        score = (
            jnp.concatenate(
                [
                    lax.dot_general(
                        query[:, c * 256 : (c + 1) * 256],
                        kbuf[r, pl.ds(0, count), c * 256 : (c + 1) * 256],
                        NT,
                        preferred_element_type=jnp.float32,
                    )
                    for c in range(chunks)
                ],
                axis=0,
            )
            * scale
        )
        usable = iota(score.shape, 1) < left[r]
        if not whole:
            score = jnp.where(usable, score, masked_score)
        top = jnp.maximum(
            jnp.max(score, axis=1, keepdims=True), jnp.max(fresh, axis=1, keepdims=True)
        )
        weight = jnp.exp(score - top)
        if not whole:
            weight = jnp.where(usable, weight, 0.0)
        fresh_weight = jnp.where(allowed, jnp.exp(fresh - top), 0.0)
        total = jnp.sum(weight, axis=1, keepdims=True) + jnp.sum(
            fresh_weight, axis=1, keepdims=True
        )
        weight = weight.astype(jnp.bfloat16)
        fresh_weight = fresh_weight.astype(jnp.bfloat16)
        shape = (all_rows, LANES)
        part = iota(shape, 1) // HEADS
        spread = jnp.zeros(shape, jnp.float32)
        for place, piece in enumerate(three_parts(top) + three_parts(total)):
            spread = jnp.where(part == place, piece, spread)
        spread = jnp.where(iota(shape, 1) % HEADS == iota(shape, 0) // steps, spread, 0.0)
        pick = iota((ROWS, all_rows), 1) % steps == iota((ROWS, all_rows), 0)
        gathered = jnp.dot(
            jnp.where(pick, 1.0, 0.0).astype(jnp.bfloat16),
            spread.astype(jnp.bfloat16),
            preferred_element_type=jnp.float32,
        )
        meta[r * steps : (r + 1) * steps, :] = gathered[:steps]
        value_move.wait()
        for c in range(chunks):
            part_rows = slice(c * rows, (c + 1) * rows)
            lanes = slice(c * 256, (c + 1) * 256)
            mixed = jnp.dot(
                weight[part_rows],
                vbuf[r, pl.ds(0, count), lanes],
                preferred_element_type=jnp.float32,
            ) + jnp.dot(
                fresh_weight[part_rows], fresh_v[:, lanes], preferred_element_type=jnp.float32
            )
            mixed = jnp.where(diag, mixed, 0.0)
            half = mixed[: 2 * steps]
            for g in range(1, group // 2):
                half = half + mixed[2 * steps * g : 2 * steps * (g + 1)]
            acc[r * steps : (r + 1) * steps, lanes] = half[:steps] + half[steps:]

    for r in range(requests):

        @pl.when(left[r] >= block)
        def _():
            one(r, block, True)

        @pl.when((left[r] > 0) & (left[r] < block))
        def _():
            one(r, SHORT, False)

        @pl.when(left[r] <= 0)
        def _():
            shape = (steps, LANES)
            hi, mid, low = three_parts(jnp.full(shape, masked_score, jnp.float32))
            part = iota(shape, 1) // HEADS
            meta[r * steps : (r + 1) * steps, :] = jnp.where(
                part == 0, hi, jnp.where(part == 1, mid, jnp.where(part == 2, low, 0.0))
            )

    out_ref[:, :width] = acc[...].astype(jnp.bfloat16)
    out_ref[:, width:] = meta[...].astype(jnp.bfloat16)


def project(
    count, ids_ref, hidden_ref, gain_ref, weight_ref, *refs
):
    parts = refs[:count]
    attn_ref, own_ref, send_ref, attn_buf, res_buf = refs[count:]
    requests, steps, width = hidden_ref.shape
    feature = attn_ref.shape[2]
    head = width // HEADS
    seq = lax.axis_index("seq")
    tp = lax.axis_index("tp")

    def moved(x, amount):
        return pltpu.roll(x, LANES - amount, 1)

    tops, totals = [], []
    for ref in parts:
        x = ref[:, width:].astype(jnp.float32)
        tops.append(x + moved(x, HEADS) + moved(x, 2 * HEADS))
        totals.append(moved(x, 3 * HEADS) + moved(x, 4 * HEADS) + moved(x, 5 * HEADS))
    overall = functools.reduce(jnp.maximum, tops)
    factors = [jnp.exp(top - overall) for top in tops]
    total = functools.reduce(jnp.add, [f * t for f, t in zip(factors, totals)])
    real = iota(total.shape, 1) < HEADS
    inverse = jnp.where(real, 1.0 / jnp.where(real, total, 1.0), 0.0)
    ratio = jnp.concatenate([jnp.where(real, f, 0.0) * inverse for f in factors], axis=0)
    expand = jnp.where(
        iota((LANES, width), 0) == iota((LANES, width), 1) // head, 1.0, 0.0
    ).astype(jnp.bfloat16)
    hi, mid, low = three_parts(ratio)
    wide = (
        jnp.dot(hi.astype(jnp.bfloat16), expand, preferred_element_type=jnp.float32)
        + jnp.dot(mid.astype(jnp.bfloat16), expand, preferred_element_type=jnp.float32)
        + jnp.dot(low.astype(jnp.bfloat16), expand, preferred_element_type=jnp.float32)
    )
    context = jnp.zeros((ROWS, width), jnp.float32)
    for b, ref in enumerate(parts):
        context = context + wide[b * ROWS : (b + 1) * ROWS] * ref[:, :width].astype(jnp.float32)
    attention = jnp.dot(
        context.astype(jnp.bfloat16), weight_ref[...], preferred_element_type=jnp.float32
    )
    hidden = [hidden_ref[r].astype(jnp.float32) for r in range(requests)]
    hidden.append(jnp.zeros((ROWS - requests * steps, width), jnp.float32))
    residual = jnp.concatenate(hidden, axis=0) + attention
    normed = (
        residual
        * lax.rsqrt(jnp.mean(residual * residual, axis=1, keepdims=True) + norm_epsilon)
        * gain_ref[...]
    )
    row = iota((ROWS, width), 0)
    lane = iota((ROWS, width), 1) - tp * ROWS
    extra = jnp.zeros((ROWS, width), jnp.float32)
    for i in range(ROWS):
        for k in range(2):
            number = jnp.float32(-1.0)
            if i < requests * steps:
                number = ids_ref[(i // steps) * 2 * steps + (i % steps) * 2 + k].astype(jnp.float32)
            if k == 0:
                first = number
        extra = jnp.where(
            lane == i,
            jnp.where(row == requests * steps, first, number),
            extra,
        )
    send_ref[...] = jnp.where(row >= requests * steps, extra, normed).astype(jnp.bfloat16)
    attn_buf[...] = attention
    res_buf[...] = residual
    lanes = pl.ds(pl.multiple_of(seq * feature, feature), feature)
    mine = attn_buf[:, lanes]
    for r in range(requests):
        attn_ref[r] = mine[r * steps : (r + 1) * steps].astype(jnp.bfloat16)
    own_ref[...] = res_buf[:, lanes]


def feed(count, capacity, steps, used, slices, router_ref, gate_ref, up_ref, down_ref, *refs):
    parts = refs[:count]
    out_ref, tokens = refs[count:]
    width = gate_ref.shape[1]
    experts = router_ref.shape[1]
    seq_size, _, _, feature = out_ref.shape
    seq = lax.axis_index("seq")
    tp = lax.axis_index("tp")
    columns = count * ROWS
    for d in range(count):
        tokens[pl.ds(pl.multiple_of((tp ^ d) * ROWS, ROWS), ROWS), :] = parts[d][...]
    ids = jnp.zeros((8, columns), jnp.float32)
    for p in range(count):
        ids = ids + tokens[p * ROWS : (p + 1) * ROWS, :columns].astype(jnp.float32)[8:]
    place = used - 8
    first = ids[place : place + 1]
    second = ids[place + 1 : place + 2]
    mine = (seq * count + tp) // slices
    mine_f = mine.astype(jnp.float32)
    hit = jnp.where((first == mine_f) | (second == mine_f), 1.0, 0.0)
    other = jnp.where(first == mine_f, second, first)
    earlier = (iota((columns, columns), 0) < iota((columns, columns), 1)) & (
        iota((columns, columns), 0) % steps == iota((columns, columns), 1) % steps
    )
    slot = jnp.dot(
        jnp.broadcast_to(hit, (ROWS, columns)).astype(jnp.bfloat16),
        jnp.where(earlier, 1.0, 0.0).astype(jnp.bfloat16),
        preferred_element_type=jnp.float32,
    )[:1]
    rows = -(-steps * capacity // ROWS) * ROWS
    row = iota((rows, columns), 0)
    choose = (
        (hit > 0.5)
        & (slot == (row % capacity).astype(jnp.float32))
        & (iota((rows, columns), 1) % steps == row // capacity)
    )
    select = jnp.where(choose, 1.0, 0.0)
    rival = jnp.sum(select * other, axis=1, keepdims=True)
    select = select.astype(jnp.bfloat16)
    buffer = jnp.dot(select, tokens[...], preferred_element_type=jnp.float32).astype(jnp.bfloat16)
    logits = jnp.dot(buffer, router_ref[...], preferred_element_type=jnp.float32)
    index = iota((rows, experts), 1)
    ahead = jnp.sum(jnp.where(index == mine, logits, 0.0), axis=1, keepdims=True)
    behind = jnp.sum(
        jnp.where(index.astype(jnp.float32) == rival, logits, 0.0), axis=1, keepdims=True
    )
    share = 1.0 / (1.0 + jnp.exp(behind - ahead))
    gate = lax.dot_general(buffer, gate_ref[...], NT, preferred_element_type=jnp.float32)
    upward = lax.dot_general(buffer, up_ref[...], NT, preferred_element_type=jnp.float32)
    inner = (jax.nn.gelu(gate) * upward).astype(jnp.bfloat16)
    produced = jnp.dot(inner, down_ref[...], preferred_element_type=jnp.float32)
    shared = (produced * share).astype(jnp.bfloat16)
    term = lax.dot_general(select, shared, TN, preferred_element_type=jnp.float32).astype(
        jnp.bfloat16
    )
    for s in range(seq_size):
        for p in range(count):
            out_ref[s, p] = term[p * ROWS : (p + 1) * ROWS, s * feature : (s + 1) * feature]


def finish(own_ref, terms_ref, out_ref):
    requests, steps, _ = out_ref.shape
    total = own_ref[...]
    mixture = terms_ref[0].astype(jnp.float32)
    for i in range(1, terms_ref.shape[0]):
        mixture = mixture + terms_ref[i].astype(jnp.float32)
    total = total + mixture
    for r in range(requests):
        out_ref[r] = total[r * steps : (r + 1) * steps].astype(jnp.bfloat16)


def body(
    hidden_in,
    new_query,
    new_key,
    new_value,
    key_cache,
    value_cache,
    lengths,
    out_weight,
    norm_gain,
    router_weight,
    expert_ids,
    gate_weight,
    up_weight,
    down_weight,
):
    requests, steps, width = hidden_in.shape
    block = key_cache.shape[1]
    seq_size = lax.axis_size("seq")
    tp_size = lax.axis_size("tp")
    feature = width // seq_size
    experts = router_weight.shape[1]
    topk = expert_ids.shape[2]
    capacity = (5 * requests * tp_size * topk + 4 * experts - 1) // (4 * experts)
    slices = seq_size * tp_size // experts
    vmem = pl.BlockSpec(memory_space=pltpu.VMEM)
    smem = pl.BlockSpec(memory_space=pltpu.SMEM)
    anywhere = pl.BlockSpec(memory_space=pl.ANY)
    limit = pltpu.CompilerParams(vmem_limit_bytes=40 * 1024 * 1024)
    message = jax.ShapeDtypeStruct((ROWS, width + LANES), jnp.bfloat16)

    part = pl.pallas_call(
        attend,
        out_shape=message,
        in_specs=[smem, vmem, vmem, vmem, anywhere, anywhere],
        out_specs=vmem,
        scratch_shapes=[
            pltpu.VMEM((requests, block, width), jnp.bfloat16),
            pltpu.VMEM((requests, block, width), jnp.bfloat16),
            pltpu.VMEM((ROWS, width), jnp.float32),
            pltpu.VMEM((ROWS, LANES), jnp.float32),
            pltpu.SemaphoreType.DMA((2, requests)),
        ],
        compiler_params=limit,
        name="attend",
    )(lengths, new_query, new_key, new_value, key_cache, value_cache)

    def swapped(x, axis, size, d):
        return lax.ppermute(x, axis, [(i, i ^ d) for i in range(size)])

    parts = [part] + [swapped(part, "seq", seq_size, d) for d in range(1, seq_size)]
    attn_out, own_residual, packed = pl.pallas_call(
        functools.partial(project, seq_size),
        out_shape=(
            jax.ShapeDtypeStruct((requests, steps, feature), jnp.bfloat16),
            jax.ShapeDtypeStruct((ROWS, feature), jnp.float32),
            jax.ShapeDtypeStruct((ROWS, width), jnp.bfloat16),
        ),
        in_specs=[smem, vmem, vmem, vmem] + [vmem] * seq_size,
        out_specs=(vmem, vmem, vmem),
        scratch_shapes=[
            pltpu.VMEM((ROWS, width), jnp.float32),
            pltpu.VMEM((ROWS, width), jnp.float32),
        ],
        compiler_params=limit,
        name="project",
    )(expert_ids.reshape(-1), hidden_in, norm_gain.reshape(1, width), out_weight, *parts)
    tokens = [packed] + [swapped(packed, "tp", tp_size, d) for d in range(1, tp_size)]
    terms = pl.pallas_call(
        functools.partial(feed, tp_size, capacity, steps, requests * steps, slices),
        out_shape=jax.ShapeDtypeStruct((seq_size, tp_size, ROWS, feature), jnp.bfloat16),
        in_specs=[vmem] * (4 + tp_size),
        out_specs=vmem,
        scratch_shapes=[pltpu.VMEM((tp_size * ROWS, width), jnp.bfloat16)],
        compiler_params=limit,
        name="feed",
    )(router_weight, gate_weight, up_weight, down_weight, *tokens)
    terms = terms.reshape(seq_size * tp_size, ROWS, feature)
    arrived = lax.all_to_all(terms, ("seq", "tp"), 0, 0, tiled=True)
    layer_out = pl.pallas_call(
        finish,
        out_shape=jax.ShapeDtypeStruct((requests, steps, feature), jnp.bfloat16),
        in_specs=[vmem, vmem],
        out_specs=vmem,
        name="finish",
    )(own_residual, arrived)
    return (attn_out, layer_out)


def solution(mesh):
    return jax.shard_map(
        body,
        mesh=mesh,
        in_specs=(
            P("tp", None, None),
            P("tp", None, None),
            P("tp", None, None),
            P("tp", None, None),
            P("tp", "seq", None),
            P("tp", "seq", None),
            P("tp"),
            P(),
            P(),
            P(),
            P("tp", None, None),
            P(("seq", "tp"), None),
            P(("seq", "tp"), None),
            P(("seq", "tp"), None),
        ),
        out_specs=(P("tp", None, "seq"), P("tp", None, "seq")),
        check_vma=False,
    )
```

time: 214 us -> 59.1 us (0.28)
  waiting for transfers between devices: 74 us -> 2.91 us
  blocking collectives: 73.8 us -> 15.4 us
  matrix products: 17.7 us -> 0 us
  starting transfers between devices: 0.08 us -> 15.3 us
  between operations: 14.9 us -> 0.73 us
  local copies, waits for them, and re-layouts: 28.3 us -> 14.6 us
  Pallas kernels: 0 us -> 9.94 us
  other arithmetic: 3.28 us -> 0 us
    unnamed x4 -> x0, waiting for transfers between devices: 74 us -> none
    all_gather x3 -> x0, blocking collectives: 48.7 us -> none  [the longest x1 22 us: body(): all_normed = lax.all_gather(normed, 'tp', axis=0, tiled=True)]
    dot_general x10 -> x0, matrix products: 17.7 us -> none  [the longest x1 4.84 us: body(): jnp.einsum('rhtp,rphe->rhte', weights.astype(jnp.bfloat16), cache_values,...]
    all_to_all x0 -> x1, blocking collectives: none -> 15.4 us  [body(): arrived = lax.all_to_all(terms, ('seq', 'tp'), 0, 0, tiled=True)]
    ppermute x0 -> x10, starting transfers between devices: none -> 15.3 us  [swapped(): return lax.ppermute(x, axis, [(i, i ^ d) for i in range(size)])]
    pmax x1 -> x0, blocking collectives: 13.3 us -> none  [body(): overall = lax.pmax(local_max, 'seq')]
    psum x1 -> x0, blocking collectives: 11.8 us -> none  [body(): lax.psum((gathered_values * factors[..., None]).astype(jnp.bfloat16), 'seq')]
    unnamed x30 -> x32, local copies, waits for them, and re-layouts: 24.6 us -> 14.5 us
  transfers between devices with their start and end apart: 2 -> 10, of which waited for: 2 -> 4; matrix products, arithmetic and copies ran while one was open for 1% -> 1% of each run, Pallas kernels for 0% -> 0%
where the time goes in v1:
time: 59.1 us; the launch traced here: 58.9 us
  blocking collectives  15.4 us (26%)
  starting transfers between devices  15.3 us (26%)
  local copies, waits for them, and re-layouts  14.6 us (25%)
  Pallas kernels  9.94 us (17%)
  waiting for transfers between devices  2.91 us (5%)
  between operations  0.73 us (1%)
    all_to_all x1, blocking collectives, body(): arrived = lax.all_to_all(terms, ('seq', 'tp'), 0, 0, tiled=True)  15.4 us
    ppermute x10, starting transfers between devices, swapped(): return lax.ppermute(x, axis, [(i, i ^ d) for i in range(size)])  15.3 us
    unnamed x32, local copies, waits for them, and re-layouts  14.5 us
    pallas_call x1, Pallas kernels, body(): pl.pallas_call(attend, out_shape=message, in_specs=[smem, vmem, vmem, vme...  4.08 us
    ppermute x10, waiting for transfers between devices, swapped(): return lax.ppermute(x, axis, [(i, i ^ d) for i in range(size)])  2.91 us
    pallas_call x1, Pallas kernels, body(): pl.pallas_call(functools.partial(feed, tp_size, capacity, steps, requests...  2.44 us
    pallas_call x1, Pallas kernels, body(): pl.pallas_call(functools.partial(project, seq_size), out_shape=(jax.Shape...  1.81 us
    pallas_call x1, Pallas kernels, body(): pl.pallas_call(finish, out_shape=jax.ShapeDtypeStruct((requests, steps, f...  1.6 us
  transfers between devices with their start and end apart: 10, of which 4 were waited for; matrix products, arithmetic and copies ran while one was open for 1% of the time, Pallas kernels for 0%

profile of v1, /device:TPU:1, one launch (start us, length us, event | category | flops | bytes accessed | tf_op | source)
XLA Modules:
  0.0 58.9 jit_solution(17829114266525329066)
XLA Ops:
  0.6 2.8 %copy-done = bf16[3,1024,1024]{2,1,0:T(8,128)(2,1)S(1)} copy-done((bf16[3,1024,1024]{2,1,0:T(8,128)(2,1)S(1)}, bf16[3,1024,1024]{2,1,0:T(8,128)(2,1)}, u32[]{:S(2)}) %copy-start) | copy-done | bytes 6291480
  3.4 2.8 %copy-done.1 = bf16[3,1024,1024]{2,1,0:T(8,128)(2,1)S(1)} copy-done((bf16[3,1024,1024]{2,1,0:T(8,128)(2,1)S(1)}, bf16[3,1024,1024]{2,1,0:T(8,128)(2,1)}, u32[]{:S(2)}) %copy-start.1) | copy-done | bytes 6291480
  6.2 0.7 %copy-done.7 = bf16[3,4,1024]{2,1,0:T(4,128)(2,1)S(1)} copy-done((bf16[3,4,1024]{2,1,0:T(4,128)(2,1)S(1)}, bf16[3,4,1024]{2,1,0:T(4,128)(2,1)}, u32[]{:S(2)}) %copy-start.7) | copy-done | bytes 24600
  6.9 0.7 %copy-done.8 = bf16[3,4,1024]{2,1,0:T(4,128)(2,1)S(1)} copy-done((bf16[3,4,1024]{2,1,0:T(4,128)(2,1)S(1)}, bf16[3,4,1024]{2,1,0:T(4,128)(2,1)}, u32[]{:S(2)}) %copy-start.8) | copy-done | bytes 24600
  7.7 0.7 %copy-done.9 = bf16[3,4,1024]{2,1,0:T(4,128)(2,1)S(1)} copy-done((bf16[3,4,1024]{2,1,0:T(4,128)(2,1)S(1)}, bf16[3,4,1024]{2,1,0:T(4,128)(2,1)}, u32[]{:S(2)}) %copy-start.9) | copy-done | bytes 24600
  8.4 0.7 %copy-done.12 = s32[3]{0:T(128)S(1)} copy-done((s32[3]{0:T(128)S(1)}, s32[3]{0:T(128)}, u32[]{:S(2)}) %copy-start.12) | copy-done | bytes 36
  9.1 4.1 %attend.1.refs_0_ = bf16[16,1152]{1,0:T(8,128)(2,1)S(1)} custom-call(s32[3]{0:T(128)S(1)} %copy-done.12, bf16[3,4,1024]{2,1,0:T(4,128)(2,1)S(1)} %copy-done.7, bf16[3,4,1024]{2,1,0:T(4,128)(2,1)S(1)} %copy-done.8, bf16[3,4,1024]{2,1,0:T(4,128)(2,1)S(1)} %copy-done.9, bf16[3,1024,1024]{2,1,0:T(8,128)(2,1)S(1)} %copy-done, bf16[3,1024,1024]{2,1,0:T(8,128)(2,1)S(1)} %copy-done.1), custom_call_target="tpu_custom_call" | custom-call | tf_op jit(solution)/shard_map/attend/pallas_call | solution.py:355
  13.2 1.5 %collective-permute-start.2 = (bf16[16,1152]{1,0:T(8,128)(2,1)S(1)}, bf16[16,1152]{1,0:T(8,128)(2,1)S(1)}, u32[]{:S(2)}, u32[]{:S(2)}) collective-permute-start(bf16[16,1152]{1,0:T(8,128)(2,1)S(1)} %attend.1.refs_0_), channel_id=1, source_target_pairs={{0,24},{8,16},{16,8},{24,0},{1,25},{9,17},{17,9},{25,1},{2,26},{10... | collective-permute-start | bytes 110600 | tf_op jit(solution)/shard_map/ppermute | solution.py:372
  14.6 0.2 collective-permute-start.1
  14.9 1.0 %collective-permute-start = (bf16[16,1152]{1,0:T(8,128)(2,1)S(1)}, bf16[16,1152]{1,0:T(8,128)(2,1)S(1)}, u32[]{:S(2)}, u32[]{:S(2)}) collective-permute-start(bf16[16,1152]{1,0:T(8,128)(2,1)S(1)} %attend.1.refs_0_), channel_id=1, source_target_pairs={{0,8},{8,0},{16,24},{24,16},{1,9},{9,1},{17,25},{25,17},{2,10},{10... | collective-permute-start | bytes 110600 | tf_op jit(solution)/shard_map/ppermute | solution.py:372
  15.9 0.1 copy.18
  16.0 0.1 reshape.13.ids_ref
  16.1 0.9 %collective-permute-done.2.refs_3_ = bf16[16,1152]{1,0:T(8,128)(2,1)S(1)} collective-permute-done((bf16[16,1152]{1,0:T(8,128)(2,1)S(1)}, bf16[16,1152]{1,0:T(8,128)(2,1)S(1)}, u32[]{:S(2)}, u32[]{:S(2)}) %collective-permute-start.2) | collective-permute-done | bytes 36896 | tf_op jit(solution)/shard_map/ppermute | solution.py:372
  17.0 1.1 %collective-permute-done.1.refs_2_ = bf16[16,1152]{1,0:T(8,128)(2,1)S(1)} collective-permute-done((bf16[16,1152]{1,0:T(8,128)(2,1)S(1)}, bf16[16,1152]{1,0:T(8,128)(2,1)S(1)}, u32[]{:S(2)}, u32[]{:S(2)}) %collective-permute-start.1) | collective-permute-done | bytes 36896 | tf_op jit(solution)/shard_map/ppermute | solution.py:372
  18.0 0.2 collective-permute-done.refs_1_
  18.2 1.6 %copy-done.5 = bf16[1024,1024]{1,0:T(8,128)(2,1)S(1)} copy-done((bf16[1024,1024]{1,0:T(8,128)(2,1)S(1)}, bf16[1024,1024]{1,0:T(8,128)(2,1)}, u32[]{:S(2)}) %copy-start.5) | copy-done | bytes 2097176
  19.8 1.8 %project.1 = (bf16[3,4,256]{2,1,0:T(4,128)(2,1)}, f32[16,256]{1,0:T(8,128)S(1)}, bf16[16,1024]{1,0:T(8,128)(2,1)S(1)}) custom-call(s32[24]{0:T(128)S(1)} %reshape.13.ids_ref, bf16[3,4,1024]{2,1,0:T(4,128)(2,1)S(1)} %copy-done.6, f32[1,1024]{1,0:T(1,128)S(1)} %bitcast.3, bf16[1024,1024]{1,0:T(8,128)(2,1)S(1)} %copy-done.5, ...), custom_call_target="tpu_custom_call" | custom-call | tf_op jit(solution)/shard_map/project/pallas_call | solution.py:375
  21.6 0.6 %copy-done.10 = f32[16,256]{1,0:T(8,128)} copy-done((f32[16,256]{1,0:T(8,128)}, f32[16,256]{1,0:T(8,128)S(1)}, u32[]{:S(2)}) %copy-start.10) | copy-done | bytes 16408
  22.2 5.3 %collective-permute-start.9 = (bf16[16,1024]{1,0:T(8,128)(2,1)S(1)}, bf16[16,1024]{1,0:T(8,128)(2,1)S(1)}, u32[]{:S(2)}, u32[]{:S(2)}) collective-permute-start(bf16[16,1024]{1,0:T(8,128)(2,1)S(1)} %get-tuple-element.7.refs_0_), channel_id=1, source_target_pairs={{0,7},{1,6},{2,5},{3,4},{4,3},{5,2},{6,1},{7,0},{8,15},{9,14},{10,... | collective-permute-start | bytes 98312 | tf_op jit(solution)/shard_map/ppermute | solution.py:372
  27.5 1.1 %collective-permute-start.8 = (bf16[16,1024]{1,0:T(8,128)(2,1)S(1)}, bf16[16,1024]{1,0:T(8,128)(2,1)S(1)}, u32[]{:S(2)}, u32[]{:S(2)}) collective-permute-start(bf16[16,1024]{1,0:T(8,128)(2,1)S(1)} %get-tuple-element.7.refs_0_), channel_id=1, source_target_pairs={{0,6},{1,7},{2,4},{3,5},{4,2},{5,3},{6,0},{7,1},{8,14},{9,15},{10,... | collective-permute-start | bytes 98312 | tf_op jit(solution)/shard_map/ppermute | solution.py:372
  28.6 2.6 %collective-permute-start.6 = (bf16[16,1024]{1,0:T(8,128)(2,1)S(1)}, bf16[16,1024]{1,0:T(8,128)(2,1)S(1)}, u32[]{:S(2)}, u32[]{:S(2)}) collective-permute-start(bf16[16,1024]{1,0:T(8,128)(2,1)S(1)} %get-tuple-element.7.refs_0_), channel_id=1, source_target_pairs={{0,4},{1,5},{2,6},{3,7},{4,0},{5,1},{6,2},{7,3},{8,12},{9,13},{10,... | collective-permute-start | bytes 98312 | tf_op jit(solution)/shard_map/ppermute | solution.py:372
  31.2 1.8 %collective-permute-start.5 = (bf16[16,1024]{1,0:T(8,128)(2,1)S(1)}, bf16[16,1024]{1,0:T(8,128)(2,1)S(1)}, u32[]{:S(2)}, u32[]{:S(2)}) collective-permute-start(bf16[16,1024]{1,0:T(8,128)(2,1)S(1)} %get-tuple-element.7.refs_0_), channel_id=1, source_target_pairs={{0,3},{1,2},{2,1},{3,0},{4,7},{5,6},{6,5},{7,4},{8,11},{9,10},{10,... | collective-permute-start | bytes 98312 | tf_op jit(solution)/shard_map/ppermute | solution.py:372
  33.0 0.0 collective-permute-start.4
  33.0 1.7 %collective-permute-start.3 = (bf16[16,1024]{1,0:T(8,128)(2,1)S(1)}, bf16[16,1024]{1,0:T(8,128)(2,1)S(1)}, u32[]{:S(2)}, u32[]{:S(2)}) collective-permute-start(bf16[16,1024]{1,0:T(8,128)(2,1)S(1)} %get-tuple-element.7.refs_0_), channel_id=1, source_target_pairs={{0,1},{1,0},{2,3},{3,2},{4,5},{5,4},{6,7},{7,6},{8,9},{9,8},{10,11... | collective-permute-start | bytes 98312 | tf_op jit(solution)/shard_map/ppermute | solution.py:372
  34.8 0.2 copy.19.router_ref
  35.0 0.0 collective-permute-done.5.refs_3_
  35.0 0.8 %collective-permute-done.4.refs_2_ = bf16[16,1024]{1,0:T(8,128)(2,1)S(1)} collective-permute-done((bf16[16,1024]{1,0:T(8,128)(2,1)S(1)}, bf16[16,1024]{1,0:T(8,128)(2,1)S(1)}, u32[]{:S(2)}, u32[]{:S(2)}) %collective-permute-start.4) | collective-permute-done | bytes 32800 | tf_op jit(solution)/shard_map/ppermute | solution.py:372
  35.8 1.8 %copy-done.3 = bf16[1408,1024]{1,0:T(8,128)(2,1)S(1)} copy-done((bf16[1408,1024]{1,0:T(8,128)(2,1)S(1)}, bf16[1408,1024]{1,0:T(8,128)(2,1)}, u32[]{:S(2)}) %copy-start.3) | copy-done | bytes 2883608
  37.6 1.8 %copy-done.4 = bf16[1408,1024]{1,0:T(8,128)(2,1)S(1)} copy-done((bf16[1408,1024]{1,0:T(8,128)(2,1)S(1)}, bf16[1408,1024]{1,0:T(8,128)(2,1)}, u32[]{:S(2)}) %copy-start.4) | copy-done | bytes 2883608
  39.4 2.4 %feed.1 = bf16[4,8,16,256]{3,2,1,0:T(8,128)(2,1)S(1)} custom-call(bf16[1024,16]{1,0:T(8,128)(2,1)S(1)} %copy.19.router_ref, bf16[1408,1024]{1,0:T(8,128)(2,1)S(1)} %copy-done.2, bf16[1408,1024]{1,0:T(8,128)(2,1)S(1)} %copy-done.3, bf16[1408,1024]{1,0:T(8,128)(2,1)S(1)} %copy-done.4, bf16[16,1024]{1,0:T(8,128)(2,1)S(1)} %get-tuple-element.7.refs_0_, ...), custom_call_target="tpu_custom_call" | custom-call | tf_op jit(solution)/shard_map/feed/pallas_call | solution.py:392
  41.9 15.4 %all_to_all.5.terms_ref = bf16[32,16,256]{2,1,0:T(8,128)(2,1)} all-to-all(bf16[32,16,256]{2,1,0:T(8,128)(2,1)S(1)} %bitcast.2), channel_id=1, replica_groups=mesh['seq'=4,'tp'=8] {'seq','tp'}, dimensions={0} | all-to-all | bytes 524288 | tf_op jit(solution)/shard_map/all_to_all | solution.py:402
  57.2 1.6 %finish.1 = bf16[3,4,256]{2,1,0:T(4,128)(2,1)} custom-call(f32[16,256]{1,0:T(8,128)} %copy-done.10, bf16[32,16,256]{2,1,0:T(8,128)(2,1)} %all_to_all.5.terms_ref), custom_call_target="tpu_custom_call" | custom-call | tf_op jit(solution)/shard_map/finish/pallas_call | solution.py:403
  (26 shorter events, 0.1 us)
Async XLA Ops:
  0.6 2.8 %copy-start = (bf16[3,1024,1024]{2,1,0:T(8,128)(2,1)S(1)}, bf16[3,1024,1024]{2,1,0:T(8,128)(2,1)}, u32[]{:S(2)}) copy-start(bf16[3,1024,1024]{2,1,0:T(8,128)(2,1)} %k_hbm.1) | copy-start | bytes 18874372
  3.4 2.8 %copy-start.1 = (bf16[3,1024,1024]{2,1,0:T(8,128)(2,1)S(1)}, bf16[3,1024,1024]{2,1,0:T(8,128)(2,1)}, u32[]{:S(2)}) copy-start(bf16[3,1024,1024]{2,1,0:T(8,128)(2,1)} %v_hbm.1) | copy-start | bytes 18874372
  6.2 0.7 %copy-start.7 = (bf16[3,4,1024]{2,1,0:T(4,128)(2,1)S(1)}, bf16[3,4,1024]{2,1,0:T(4,128)(2,1)}, u32[]{:S(2)}) copy-start(bf16[3,4,1024]{2,1,0:T(4,128)(2,1)} %q_ref.1) | copy-start | bytes 73732
  6.9 0.7 %copy-start.8 = (bf16[3,4,1024]{2,1,0:T(4,128)(2,1)S(1)}, bf16[3,4,1024]{2,1,0:T(4,128)(2,1)}, u32[]{:S(2)}) copy-start(bf16[3,4,1024]{2,1,0:T(4,128)(2,1)} %nk_ref.1) | copy-start | bytes 73732
  7.7 0.7 %copy-start.9 = (bf16[3,4,1024]{2,1,0:T(4,128)(2,1)S(1)}, bf16[3,4,1024]{2,1,0:T(4,128)(2,1)}, u32[]{:S(2)}) copy-start(bf16[3,4,1024]{2,1,0:T(4,128)(2,1)} %nv_ref.1) | copy-start | bytes 73732
  8.4 0.7 %copy-start.12 = (s32[3]{0:T(128)S(1)}, s32[3]{0:T(128)}, u32[]{:S(2)}) copy-start(s32[3]{0:T(128)} %lens.1) | copy-start | bytes 40
  9.1 6.8 %copy-start.14 = (s32[3,4,2]{1,2,0:T(2,128)S(1)}, s32[3,4,2]{1,2,0:T(2,128)}, u32[]{:S(2)}) copy-start(s32[3,4,2]{1,2,0:T(2,128)} %param.24) | copy-start | bytes 292
  9.1 9.1 %copy-start.6 = (bf16[3,4,1024]{2,1,0:T(4,128)(2,1)S(1)}, bf16[3,4,1024]{2,1,0:T(4,128)(2,1)}, u32[]{:S(2)}) copy-start(bf16[3,4,1024]{2,1,0:T(4,128)(2,1)} %hidden_ref.1) | copy-start | bytes 73732
  9.1 9.1 %copy-start.11 = (f32[1024]{0:T(1024)S(1)}, f32[1024]{0:T(1024)}, u32[]{:S(2)}) copy-start(f32[1024]{0:T(1024)} %param.22) | copy-start | bytes 12292
  9.1 25.7 %copy-start.13 = (bf16[1024,16]{0,1:T(8,128)(2,1)S(1)}, bf16[1024,16]{0,1:T(8,128)(2,1)}, u32[]{:S(2)}) copy-start(bf16[1024,16]{0,1:T(8,128)(2,1)} %param.23) | copy-start | bytes 98308
  9.1 26.7 %copy-start.2 = (bf16[1408,1024]{1,0:T(8,128)(2,1)S(1)}, bf16[1408,1024]{1,0:T(8,128)(2,1)}, u32[]{:S(2)}) copy-start(bf16[1408,1024]{1,0:T(8,128)(2,1)} %gate_ref.1) | copy-start | bytes 8650756
  13.2 3.8 %collective-permute-start.2 = (bf16[16,1152]{1,0:T(8,128)(2,1)S(1)}, bf16[16,1152]{1,0:T(8,128)(2,1)S(1)}, u32[]{:S(2)}, u32[]{:S(2)}) collective-permute-start(bf16[16,1152]{1,0:T(8,128)(2,1)S(1)} %attend.1.refs_0_), channel_id=1, source_target_pairs={{0,24},{8,16},{16,8},{24,0},{1,25},{9,17},{17,9},{25,1},{2,26},{10... | collective-permute-start | bytes 110600 | tf_op jit(solution)/shard_map/ppermute | solution.py:372
  14.6 3.4 %collective-permute-start.1 = (bf16[16,1152]{1,0:T(8,128)(2,1)S(1)}, bf16[16,1152]{1,0:T(8,128)(2,1)S(1)}, u32[]{:S(2)}, u32[]{:S(2)}) collective-permute-start(bf16[16,1152]{1,0:T(8,128)(2,1)S(1)} %attend.1.refs_0_), channel_id=1, source_target_pairs={{0,16},{8,24},{16,0},{24,8},{1,17},{9,25},{17,1},{25,9},{2,18},{10... | collective-permute-start | bytes 110600 | tf_op jit(solution)/shard_map/ppermute | solution.py:372
  14.9 3.3 %collective-permute-start = (bf16[16,1152]{1,0:T(8,128)(2,1)S(1)}, bf16[16,1152]{1,0:T(8,128)(2,1)S(1)}, u32[]{:S(2)}, u32[]{:S(2)}) collective-permute-start(bf16[16,1152]{1,0:T(8,128)(2,1)S(1)} %attend.1.refs_0_), channel_id=1, source_target_pairs={{0,8},{8,0},{16,24},{24,16},{1,9},{9,1},{17,25},{25,17},{2,10},{10... | collective-permute-start | bytes 110600 | tf_op jit(solution)/shard_map/ppermute | solution.py:372
  18.2 1.6 %copy-start.5 = (bf16[1024,1024]{1,0:T(8,128)(2,1)S(1)}, bf16[1024,1024]{1,0:T(8,128)(2,1)}, u32[]{:S(2)}) copy-start(bf16[1024,1024]{1,0:T(8,128)(2,1)} %weight_ref.1) | copy-start | bytes 6291460
  21.6 0.6 %copy-start.10 = (f32[16,256]{1,0:T(8,128)}, f32[16,256]{1,0:T(8,128)S(1)}, u32[]{:S(2)}) copy-start(f32[16,256]{1,0:T(8,128)S(1)} %get-tuple-element.6.own_ref) | copy-start | bytes 49156
  22.2 10.8 %collective-permute-start.9 = (bf16[16,1024]{1,0:T(8,128)(2,1)S(1)}, bf16[16,1024]{1,0:T(8,128)(2,1)S(1)}, u32[]{:S(2)}, u32[]{:S(2)}) collective-permute-start(bf16[16,1024]{1,0:T(8,128)(2,1)S(1)} %get-tuple-element.7.refs_0_), channel_id=1, source_target_pairs={{0,7},{1,6},{2,5},{3,4},{4,3},{5,2},{6,1},{7,0},{8,15},{9,14},{10,... | collective-permute-start | bytes 98312 | tf_op jit(solution)/shard_map/ppermute | solution.py:372
  27.5 5.6 %collective-permute-start.8 = (bf16[16,1024]{1,0:T(8,128)(2,1)S(1)}, bf16[16,1024]{1,0:T(8,128)(2,1)S(1)}, u32[]{:S(2)}, u32[]{:S(2)}) collective-permute-start(bf16[16,1024]{1,0:T(8,128)(2,1)S(1)} %get-tuple-element.7.refs_0_), channel_id=1, source_target_pairs={{0,6},{1,7},{2,4},{3,5},{4,2},{5,3},{6,0},{7,1},{8,14},{9,15},{10,... | collective-permute-start | bytes 98312 | tf_op jit(solution)/shard_map/ppermute | solution.py:372
  28.6 6.4 %collective-permute-start.7 = (bf16[16,1024]{1,0:T(8,128)(2,1)S(1)}, bf16[16,1024]{1,0:T(8,128)(2,1)S(1)}, u32[]{:S(2)}, u32[]{:S(2)}) collective-permute-start(bf16[16,1024]{1,0:T(8,128)(2,1)S(1)} %get-tuple-element.7.refs_0_), channel_id=1, source_target_pairs={{0,5},{1,4},{2,7},{3,6},{4,1},{5,0},{6,3},{7,2},{8,13},{9,12},{10,... | collective-permute-start | bytes 98312 | tf_op jit(solution)/shard_map/ppermute | solution.py:372
  28.6 6.4 %collective-permute-start.6 = (bf16[16,1024]{1,0:T(8,128)(2,1)S(1)}, bf16[16,1024]{1,0:T(8,128)(2,1)S(1)}, u32[]{:S(2)}, u32[]{:S(2)}) collective-permute-start(bf16[16,1024]{1,0:T(8,128)(2,1)S(1)} %get-tuple-element.7.refs_0_), channel_id=1, source_target_pairs={{0,4},{1,5},{2,6},{3,7},{4,0},{5,1},{6,2},{7,3},{8,12},{9,13},{10,... | collective-permute-start | bytes 98312 | tf_op jit(solution)/shard_map/ppermute | solution.py:372
  31.2 3.8 %collective-permute-start.5 = (bf16[16,1024]{1,0:T(8,128)(2,1)S(1)}, bf16[16,1024]{1,0:T(8,128)(2,1)S(1)}, u32[]{:S(2)}, u32[]{:S(2)}) collective-permute-start(bf16[16,1024]{1,0:T(8,128)(2,1)S(1)} %get-tuple-element.7.refs_0_), channel_id=1, source_target_pairs={{0,3},{1,2},{2,1},{3,0},{4,7},{5,6},{6,5},{7,4},{8,11},{9,10},{10,... | collective-permute-start | bytes 98312 | tf_op jit(solution)/shard_map/ppermute | solution.py:372
  33.0 2.8 %collective-permute-start.4 = (bf16[16,1024]{1,0:T(8,128)(2,1)S(1)}, bf16[16,1024]{1,0:T(8,128)(2,1)S(1)}, u32[]{:S(2)}, u32[]{:S(2)}) collective-permute-start(bf16[16,1024]{1,0:T(8,128)(2,1)S(1)} %get-tuple-element.7.refs_0_), channel_id=1, source_target_pairs={{0,2},{1,3},{2,0},{3,1},{4,6},{5,7},{6,4},{7,5},{8,10},{9,11},{10,... | collective-permute-start | bytes 98312 | tf_op jit(solution)/shard_map/ppermute | solution.py:372
  33.0 2.7 %collective-permute-start.3 = (bf16[16,1024]{1,0:T(8,128)(2,1)S(1)}, bf16[16,1024]{1,0:T(8,128)(2,1)S(1)}, u32[]{:S(2)}, u32[]{:S(2)}) collective-permute-start(bf16[16,1024]{1,0:T(8,128)(2,1)S(1)} %get-tuple-element.7.refs_0_), channel_id=1, source_target_pairs={{0,1},{1,0},{2,3},{3,2},{4,5},{5,4},{6,7},{7,6},{8,9},{9,8},{10,11... | collective-permute-start | bytes 98312 | tf_op jit(solution)/shard_map/ppermute | solution.py:372
  35.8 1.8 %copy-start.3 = (bf16[1408,1024]{1,0:T(8,128)(2,1)S(1)}, bf16[1408,1024]{1,0:T(8,128)(2,1)}, u32[]{:S(2)}) copy-start(bf16[1408,1024]{1,0:T(8,128)(2,1)} %up_ref.1) | copy-start | bytes 8650756
  37.6 1.8 %copy-start.4 = (bf16[1408,1024]{1,0:T(8,128)(2,1)S(1)}, bf16[1408,1024]{1,0:T(8,128)(2,1)}, u32[]{:S(2)}) copy-start(bf16[1408,1024]{1,0:T(8,128)(2,1)} %down_ref.1) | copy-start | bytes 8650756

commit v2 on v1

--- a/solution.py
+++ b/solution.py
@@ -31,7 +31,10 @@
     return jnp.concatenate([x] * times, axis=0)
 
 
-def attend(lens, q_ref, nk_ref, nv_ref, k_hbm, v_hbm, out_ref, kbuf, vbuf, acc, meta, sems):
+def attend(
+    lens_hbm, q_hbm, nk_hbm, nv_hbm, k_hbm, v_hbm, out_ref,
+    lens, q_ref, nk_ref, nv_ref, kbuf, vbuf, acc, meta, sems, small_sems,
+):
     requests, block, width = k_hbm.shape
     steps = q_ref.shape[1]
     head = width // HEADS
@@ -51,6 +54,15 @@
             )
         return pair
 
+    small = [
+        pltpu.make_async_copy(src, dst, small_sems.at[i])
+        for i, (src, dst) in enumerate(
+            ((lens_hbm, lens), (q_hbm, q_ref), (nk_hbm, nk_ref), (nv_hbm, nv_ref))
+        )
+    ]
+    for move in small:
+        move.start()
+    small[0].wait()
     left = [lens[r] - seq * block for r in range(requests)]
     for r in range(requests):
 
@@ -67,6 +79,8 @@
     acc[...] = jnp.zeros_like(acc)
     meta[...] = jnp.where(iota(meta.shape, 1) // HEADS == 3, 1.0, 0.0)
 
+    for move in small[1:]:
+        move.wait()
     diag = iota((rows, 256), 0) // steps == iota((rows, 256), 1) // head
     diag_all = iota((rows, width), 0) // steps == (iota((rows, width), 1) % 256) // head
     all_rows = chunks * rows
@@ -173,15 +187,16 @@
                 part == 0, hi, jnp.where(part == 1, mid, jnp.where(part == 2, low, 0.0))
             )
 
-    out_ref[:, :width] = acc[...].astype(jnp.bfloat16)
-    out_ref[:, width:] = meta[...].astype(jnp.bfloat16)
+    for b in range(out_ref.shape[0]):
+        out_ref[b, :, :width] = acc[...].astype(jnp.bfloat16)
+        out_ref[b, :, width:] = meta[...].astype(jnp.bfloat16)
 
 
 def project(
-    count, ids_ref, hidden_ref, gain_ref, weight_ref, *refs
+    ids_ref, hidden_ref, gain_ref, weight_ref, parts_ref,
+    attn_ref, own_ref, send_ref, attn_buf, res_buf,
 ):
-    parts = refs[:count]
-    attn_ref, own_ref, send_ref, attn_buf, res_buf = refs[count:]
+    parts = [parts_ref.at[b] for b in range(parts_ref.shape[0])]
     requests, steps, width = hidden_ref.shape
     feature = attn_ref.shape[2]
     head = width // HEADS
@@ -225,22 +240,21 @@
         * lax.rsqrt(jnp.mean(residual * residual, axis=1, keepdims=True) + norm_epsilon)
         * gain_ref[...]
     )
-    row = iota((ROWS, width), 0)
-    lane = iota((ROWS, width), 1) - tp * ROWS
-    extra = jnp.zeros((ROWS, width), jnp.float32)
-    for i in range(ROWS):
-        for k in range(2):
-            number = jnp.float32(-1.0)
-            if i < requests * steps:
-                number = ids_ref[(i // steps) * 2 * steps + (i % steps) * 2 + k].astype(jnp.float32)
-            if k == 0:
-                first = number
-        extra = jnp.where(
-            lane == i,
-            jnp.where(row == requests * steps, first, number),
-            extra,
-        )
-    send_ref[...] = jnp.where(row >= requests * steps, extra, normed).astype(jnp.bfloat16)
+    columns = send_ref.shape[0] * ROWS
+    row = iota((ROWS, columns), 0)
+    lane = iota((ROWS, columns), 1) - tp * ROWS
+    extra = jnp.where((lane >= 0) & (lane < ROWS), -1.0, 0.0)
+    for i in range(requests * steps):
+        first, second = [
+            ids_ref[i // steps, k, i % steps].astype(jnp.float32) for k in range(2)
+        ]
+        extra = jnp.where(lane == i, jnp.where(row == requests * steps, first, second), extra)
+    tail = row >= requests * steps
+    message = jnp.concatenate(
+        [jnp.where(tail, extra, normed[:, :columns]), normed[:, columns:]], axis=1
+    ).astype(jnp.bfloat16)
+    for p in range(send_ref.shape[0]):
+        send_ref[p] = message
     attn_buf[...] = attention
     res_buf[...] = residual
     lanes = pl.ds(pl.multiple_of(seq * feature, feature), feature)
@@ -250,17 +264,16 @@
     own_ref[...] = res_buf[:, lanes]
 
 
-def feed(count, capacity, steps, used, slices, router_ref, gate_ref, up_ref, down_ref, *refs):
-    parts = refs[:count]
-    out_ref, tokens = refs[count:]
+def feed(
+    capacity, steps, used, slices, router_ref, gate_ref, up_ref, down_ref, tokens, out_ref
+):
+    count = tokens.shape[0] // ROWS
     width = gate_ref.shape[1]
-    experts = router_ref.shape[1]
+    experts = router_ref.shape[0]
     seq_size, _, _, feature = out_ref.shape
     seq = lax.axis_index("seq")
     tp = lax.axis_index("tp")
     columns = count * ROWS
-    for d in range(count):
-        tokens[pl.ds(pl.multiple_of((tp ^ d) * ROWS, ROWS), ROWS), :] = parts[d][...]
     ids = jnp.zeros((8, columns), jnp.float32)
     for p in range(count):
         ids = ids + tokens[p * ROWS : (p + 1) * ROWS, :columns].astype(jnp.float32)[8:]
@@ -290,7 +303,7 @@
     rival = jnp.sum(select * other, axis=1, keepdims=True)
     select = select.astype(jnp.bfloat16)
     buffer = jnp.dot(select, tokens[...], preferred_element_type=jnp.float32).astype(jnp.bfloat16)
-    logits = jnp.dot(buffer, router_ref[...], preferred_element_type=jnp.float32)
+    logits = lax.dot_general(buffer, router_ref[...], NT, preferred_element_type=jnp.float32)
     index = iota((rows, experts), 1)
     ahead = jnp.sum(jnp.where(index == mine, logits, 0.0), axis=1, keepdims=True)
     behind = jnp.sum(
@@ -348,56 +361,63 @@
     slices = seq_size * tp_size // experts
     vmem = pl.BlockSpec(memory_space=pltpu.VMEM)
     smem = pl.BlockSpec(memory_space=pltpu.SMEM)
-    anywhere = pl.BlockSpec(memory_space=pl.ANY)
-    limit = pltpu.CompilerParams(vmem_limit_bytes=40 * 1024 * 1024)
-    message = jax.ShapeDtypeStruct((ROWS, width + LANES), jnp.bfloat16)
-
+    hbm = pl.BlockSpec(memory_space=pltpu.HBM)
+
+    def limit(mebibytes):
+        return pltpu.CompilerParams(vmem_limit_bytes=mebibytes * 1024 * 1024)
+
+    small = pltpu.VMEM((requests, steps, width), jnp.bfloat16)
     part = pl.pallas_call(
         attend,
-        out_shape=message,
-        in_specs=[smem, vmem, vmem, vmem, anywhere, anywhere],
+        out_shape=jax.ShapeDtypeStruct((seq_size, ROWS, width + LANES), jnp.bfloat16),
+        in_specs=[hbm] * 6,
         out_specs=vmem,
         scratch_shapes=[
+            pltpu.SMEM((requests,), jnp.int32),
+            small,
+            small,
+            small,
             pltpu.VMEM((requests, block, width), jnp.bfloat16),
             pltpu.VMEM((requests, block, width), jnp.bfloat16),
             pltpu.VMEM((ROWS, width), jnp.float32),
             pltpu.VMEM((ROWS, LANES), jnp.float32),
             pltpu.SemaphoreType.DMA((2, requests)),
+            pltpu.SemaphoreType.DMA((4,)),
         ],
-        compiler_params=limit,
+        compiler_params=limit(20),
         name="attend",
-    )(lengths, new_query, new_key, new_value, key_cache, value_cache)
-
-    def swapped(x, axis, size, d):
-        return lax.ppermute(x, axis, [(i, i ^ d) for i in range(size)])
-
-    parts = [part] + [swapped(part, "seq", seq_size, d) for d in range(1, seq_size)]
+    )(
+        *[
+            pltpu.with_memory_space_constraint(x, pltpu.HBM)
+            for x in (lengths, new_query, new_key, new_value, key_cache, value_cache)
+        ]
+    )
+    parts = lax.all_to_all(part, "seq", 0, 0, tiled=True)
     attn_out, own_residual, packed = pl.pallas_call(
-        functools.partial(project, seq_size),
+        project,
         out_shape=(
             jax.ShapeDtypeStruct((requests, steps, feature), jnp.bfloat16),
             jax.ShapeDtypeStruct((ROWS, feature), jnp.float32),
-            jax.ShapeDtypeStruct((ROWS, width), jnp.bfloat16),
+            jax.ShapeDtypeStruct((tp_size, ROWS, width), jnp.bfloat16),
         ),
-        in_specs=[smem, vmem, vmem, vmem] + [vmem] * seq_size,
+        in_specs=[smem, vmem, vmem, vmem, vmem],
         out_specs=(vmem, vmem, vmem),
         scratch_shapes=[
             pltpu.VMEM((ROWS, width), jnp.float32),
             pltpu.VMEM((ROWS, width), jnp.float32),
         ],
-        compiler_params=limit,
+        compiler_params=limit(8),
         name="project",
-    )(expert_ids.reshape(-1), hidden_in, norm_gain.reshape(1, width), out_weight, *parts)
-    tokens = [packed] + [swapped(packed, "tp", tp_size, d) for d in range(1, tp_size)]
+    )(expert_ids.transpose(0, 2, 1), hidden_in, norm_gain.reshape(1, width), out_weight, parts)
+    tokens = lax.all_to_all(packed, "tp", 0, 0, tiled=True).reshape(tp_size * ROWS, width)
     terms = pl.pallas_call(
-        functools.partial(feed, tp_size, capacity, steps, requests * steps, slices),
+        functools.partial(feed, capacity, steps, requests * steps, slices),
         out_shape=jax.ShapeDtypeStruct((seq_size, tp_size, ROWS, feature), jnp.bfloat16),
-        in_specs=[vmem] * (4 + tp_size),
+        in_specs=[vmem] * 5,
         out_specs=vmem,
-        scratch_shapes=[pltpu.VMEM((tp_size * ROWS, width), jnp.bfloat16)],
-        compiler_params=limit,
+        compiler_params=limit(16),
         name="feed",
-    )(router_weight, gate_weight, up_weight, down_weight, *tokens)
+    )(router_weight.T, gate_weight, up_weight, down_weight, tokens)
     terms = terms.reshape(seq_size * tp_size, ROWS, feature)
     arrived = lax.all_to_all(terms, ("seq", "tp"), 0, 0, tiled=True)
     layer_out = pl.pallas_call(

time: 59.1 us -> 49.2 us (0.83); the launches traced: 58.9 us -> 48.3 us
  blocking collectives: 15.4 us -> 36.3 us
  starting transfers between devices: 15.3 us -> 0 us
  local copies, waits for them, and re-layouts: 14.6 us -> 0.04 us
  waiting for transfers between devices: 2.91 us -> 0 us
  Pallas kernels: 9.94 us -> 11.1 us
    all_to_all x0 -> x2, blocking collectives: none -> 22.7 us  [the longest x1 14.9 us: body(): lax.all_to_all(packed, 'tp', 0, 0, tiled=True)]
    ppermute x10 -> x0, starting transfers between devices: 15.3 us -> none  [swapped(): return lax.ppermute(x, axis, [(i, i ^ d) for i in range(size)])]
    unnamed x32 -> x18, local copies, waits for them, and re-layouts: 14.5 us -> 0.04 us
    ppermute x10 -> x0, waiting for transfers between devices: 2.91 us -> none  [swapped(): return lax.ppermute(x, axis, [(i, i ^ d) for i in range(size)])]
    all_to_all x1, blocking collectives: 15.4 us -> 13.7 us  [body(): arrived = lax.all_to_all(terms, ('seq', 'tp'), 0, 0, tiled=True)]
    pallas_call x3, Pallas kernels: 8.33 us -> 9.53 us  [the longest x1 5.26 us: body(): pl.pallas_call(attend, out_shape=jax.ShapeDtypeStruct((seq_size, ROWS, wi...]
  transfers between devices with their start and end apart: 10 -> 0, of which waited for: 4 -> 0; matrix products, arithmetic and copies ran while one was open for 1% -> 0% of each run, Pallas kernels for 0% -> 0%
where the time goes in v2:
time: 49.2 us; the launch traced here: 48.3 us
  blocking collectives  36.3 us (74%)
  Pallas kernels  11.1 us (23%)
  between operations  0.75 us (2%)
    all_to_all x1, blocking collectives, body(): lax.all_to_all(packed, 'tp', 0, 0, tiled=True)  14.9 us
    all_to_all x1, blocking collectives, body(): arrived = lax.all_to_all(terms, ('seq', 'tp'), 0, 0, tiled=True)  13.7 us
    all_to_all x1, blocking collectives, body(): parts = lax.all_to_all(part, 'seq', 0, 0, tiled=True)  7.77 us
    pallas_call x1, Pallas kernels, body(): pl.pallas_call(attend, out_shape=jax.ShapeDtypeStruct((seq_size, ROWS, wi...  5.26 us
    pallas_call x1, Pallas kernels, body(): pl.pallas_call(functools.partial(feed, capacity, steps, requests * steps,...  2.41 us
    pallas_call x1, Pallas kernels, body(): pl.pallas_call(project, out_shape=(jax.ShapeDtypeStruct((requests, steps,...  1.87 us
    pallas_call x1, Pallas kernels, body(): pl.pallas_call(finish, out_shape=jax.ShapeDtypeStruct((requests, steps, f...  1.6 us

profile of v2, /device:TPU:1, one launch (start us, length us, event | category | flops | bytes accessed | tf_op | source)
XLA Modules:
  0.0 48.3 jit_solution(13799174739023421671)
XLA Ops:
  0.6 0.0 copy-start.8
  0.6 0.0 copy-start.7
  0.7 0.0 copy-start.3
  0.7 0.0 copy-start.5
  0.7 0.0 copy-start.1
  0.7 0.0 copy-start.2
  0.7 5.3 %attend.1 = bf16[4,16,1152]{2,1,0:T(8,128)(2,1)S(1)} custom-call(s32[3]{0:T(128)} %lens_hbm.1, bf16[3,4,1024]{2,1,0:T(4,128)(2,1)} %q_hbm.1, bf16[3,4,1024]{2,1,0:T(4,128)(2,1)} %nk_hbm.1, bf16[3,4,1024]{2,1,0:T(4,128)(2,1)} %nv_hbm.1, bf16[3,1024,1024]{2,1,0:T(8,128)(2,1)} %k_hbm.1, bf16[3,1024,1024]{2,1,0:T(8,128)(2,1)} %v_hbm.1), custom_call_target="tpu_custom_call" | custom-call | tf_op jit(solution)/shard_map/attend/pallas_call | solution.py:370
  6.0 0.0 copy-start
  6.0 0.0 copy-start.4
  6.0 7.8 %all_to_all.15.parts_ref = bf16[4,16,1152]{2,1,0:T(8,128)(2,1)S(1)} all-to-all(bf16[4,16,1152]{2,1,0:T(8,128)(2,1)S(1)} %attend.1), channel_id=1, replica_groups=mesh['seq'=4,'tp'=8] {'seq'}, dimensions={0} | all-to-all | bytes 294912 | tf_op jit(solution)/shard_map/all_to_all | solution.py:395
  13.8 0.0 copy-done.8
  13.8 0.0 copy-done.7
  13.8 0.0 copy-done.3
  13.8 0.0 copy-done.5
  13.8 1.9 %project.1 = (bf16[3,4,256]{2,1,0:T(4,128)(2,1)}, f32[16,256]{1,0:T(8,128)S(1)}, bf16[8,16,1024]{2,1,0:T(8,128)(2,1)S(1)}) custom-call(s32[3,2,4]{2,1,0:T(2,128)S(1)} %bitcast.9, bf16[3,4,1024]{2,1,0:T(4,128)(2,1)S(1)} %copy-done.5, f32[1,1024]{1,0:T(1,128)S(1)} %bitcast.8, bf16[1024,1024]{1,0:T(8,128)(2,1)S(1)} %copy-done.3, ...), custom_call_target="tpu_custom_call" | custom-call | tf_op jit(solution)/shard_map/project/pallas_call | solution.py:396
  15.6 0.0 copy-start.6
  15.6 14.9 %all_to_all.16 = bf16[8,16,1024]{2,1,0:T(8,128)(2,1)S(1)} all-to-all(bf16[8,16,1024]{2,1,0:T(8,128)(2,1)S(1)} %get-tuple-element.7), channel_id=1, replica_groups=mesh['seq'=4,'tp'=8] {'tp'}, dimensions={0} | all-to-all | bytes 524288 | tf_op jit(solution)/shard_map/all_to_all | solution.py:412
  30.5 0.0 copy-done.6
  30.5 0.0 copy-done.1
  30.5 0.0 copy-done.2
  30.5 0.0 copy-done
  30.6 0.0 copy-done.4
  30.6 2.4 %feed.1 = bf16[4,8,16,256]{3,2,1,0:T(8,128)(2,1)S(1)} custom-call(bf16[16,1024]{1,0:T(8,128)(2,1)S(1)} %bitcast.7, bf16[1408,1024]{1,0:T(8,128)(2,1)S(1)} %copy-done, bf16[1408,1024]{1,0:T(8,128)(2,1)S(1)} %copy-done.1, bf16[1408,1024]{1,0:T(8,128)(2,1)S(1)} %copy-done.2, bf16[128,1024]{1,0:T(8,128)(2,1)S(1)} %bitcast.5), custom_call_target="tpu_custom_call" | custom-call | tf_op jit(solution)/shard_map/feed/pallas_call | solution.py:413
  33.0 13.7 %all_to_all.17.terms_ref = bf16[32,16,256]{2,1,0:T(8,128)(2,1)} all-to-all(bf16[32,16,256]{2,1,0:T(8,128)(2,1)S(1)} %bitcast.6), channel_id=1, replica_groups=mesh['seq'=4,'tp'=8] {'seq','tp'}, dimensions={0} | all-to-all | bytes 524288 | tf_op jit(solution)/shard_map/all_to_all | solution.py:422
  46.7 1.6 %finish.1 = bf16[3,4,256]{2,1,0:T(4,128)(2,1)} custom-call(f32[16,256]{1,0:T(8,128)} %copy-done.6, bf16[32,16,256]{2,1,0:T(8,128)(2,1)} %all_to_all.17.terms_ref), custom_call_target="tpu_custom_call" | custom-call | tf_op jit(solution)/shard_map/finish/pallas_call | solution.py:423
Async XLA Ops:
  0.6 13.1 %copy-start.8 = (s32[3,4,2]{1,2,0:T(2,128)S(1)}, s32[3,4,2]{1,2,0:T(2,128)}, u32[]{:S(2)}) copy-start(s32[3,4,2]{1,2,0:T(2,128)} %param.24) | copy-start | bytes 292
  0.6 13.1 %copy-start.7 = (f32[1024]{0:T(1024)S(1)}, f32[1024]{0:T(1024)}, u32[]{:S(2)}) copy-start(f32[1024]{0:T(1024)} %param.22) | copy-start | bytes 12292
  0.7 13.1 %copy-start.3 = (bf16[1024,1024]{1,0:T(8,128)(2,1)S(1)}, bf16[1024,1024]{1,0:T(8,128)(2,1)}, u32[]{:S(2)}) copy-start(bf16[1024,1024]{1,0:T(8,128)(2,1)} %weight_ref.1) | copy-start | bytes 6291460
  0.7 13.1 %copy-start.5 = (bf16[3,4,1024]{2,1,0:T(4,128)(2,1)S(1)}, bf16[3,4,1024]{2,1,0:T(4,128)(2,1)}, u32[]{:S(2)}) copy-start(bf16[3,4,1024]{2,1,0:T(4,128)(2,1)} %hidden_ref.1) | copy-start | bytes 73732
  0.7 29.9 %copy-start.1 = (bf16[1408,1024]{1,0:T(8,128)(2,1)S(1)}, bf16[1408,1024]{1,0:T(8,128)(2,1)}, u32[]{:S(2)}) copy-start(bf16[1408,1024]{1,0:T(8,128)(2,1)} %up_ref.1) | copy-start | bytes 8650756
  0.7 29.9 %copy-start.2 = (bf16[1408,1024]{1,0:T(8,128)(2,1)S(1)}, bf16[1408,1024]{1,0:T(8,128)(2,1)}, u32[]{:S(2)}) copy-start(bf16[1408,1024]{1,0:T(8,128)(2,1)} %down_ref.1) | copy-start | bytes 8650756
  6.0 24.6 %copy-start = (bf16[1408,1024]{1,0:T(8,128)(2,1)S(1)}, bf16[1408,1024]{1,0:T(8,128)(2,1)}, u32[]{:S(2)}) copy-start(bf16[1408,1024]{1,0:T(8,128)(2,1)} %gate_ref.1) | copy-start | bytes 8650756
  6.0 24.6 %copy-start.4 = (bf16[1024,16]{0,1:T(8,128)(2,1)S(1)}, bf16[1024,16]{0,1:T(8,128)(2,1)}, u32[]{:S(2)}) copy-start(bf16[1024,16]{0,1:T(8,128)(2,1)} %param.23) | copy-start | bytes 98308
  15.6 14.9 %copy-start.6 = (f32[16,256]{1,0:T(8,128)}, f32[16,256]{1,0:T(8,128)S(1)}, u32[]{:S(2)}) copy-start(f32[16,256]{1,0:T(8,128)S(1)} %get-tuple-element.6.own_ref) | copy-start | bytes 49156

commit v3 on v2

--- a/solution.py
+++ b/solution.py
@@ -187,16 +187,13 @@
                 part == 0, hi, jnp.where(part == 1, mid, jnp.where(part == 2, low, 0.0))
             )
 
-    for b in range(out_ref.shape[0]):
-        out_ref[b, :, :width] = acc[...].astype(jnp.bfloat16)
-        out_ref[b, :, width:] = meta[...].astype(jnp.bfloat16)
-
-
-def project(
-    ids_ref, hidden_ref, gain_ref, weight_ref, parts_ref,
-    attn_ref, own_ref, send_ref, attn_buf, res_buf,
-):
-    parts = [parts_ref.at[b] for b in range(parts_ref.shape[0])]
+    out_ref[:, :width] = acc[...].astype(jnp.bfloat16)
+    out_ref[:, width:] = meta[...].astype(jnp.bfloat16)
+
+
+def project(count, columns, ids_ref, hidden_ref, gain_ref, weight_ref, *refs):
+    parts = refs[:count]
+    attn_ref, own_ref, send_ref, attn_buf, res_buf = refs[count:]
     requests, steps, width = hidden_ref.shape
     feature = attn_ref.shape[2]
     head = width // HEADS
@@ -218,14 +215,14 @@
     inverse = jnp.where(real, 1.0 / jnp.where(real, total, 1.0), 0.0)
     ratio = jnp.concatenate([jnp.where(real, f, 0.0) * inverse for f in factors], axis=0)
     expand = jnp.where(
-        iota((LANES, width), 0) == iota((LANES, width), 1) // head, 1.0, 0.0
+        (iota((LANES, width), 0) % HEADS == iota((LANES, width), 1) // head)
+        & (iota((LANES, width), 0) < 3 * HEADS),
+        1.0,
+        0.0,
     ).astype(jnp.bfloat16)
     hi, mid, low = three_parts(ratio)
-    wide = (
-        jnp.dot(hi.astype(jnp.bfloat16), expand, preferred_element_type=jnp.float32)
-        + jnp.dot(mid.astype(jnp.bfloat16), expand, preferred_element_type=jnp.float32)
-        + jnp.dot(low.astype(jnp.bfloat16), expand, preferred_element_type=jnp.float32)
-    )
+    packed = hi + pltpu.roll(mid, HEADS, 1) + pltpu.roll(low, 2 * HEADS, 1)
+    wide = jnp.dot(packed.astype(jnp.bfloat16), expand, preferred_element_type=jnp.float32)
     context = jnp.zeros((ROWS, width), jnp.float32)
     for b, ref in enumerate(parts):
         context = context + wide[b * ROWS : (b + 1) * ROWS] * ref[:, :width].astype(jnp.float32)
@@ -240,7 +237,6 @@
         * lax.rsqrt(jnp.mean(residual * residual, axis=1, keepdims=True) + norm_epsilon)
         * gain_ref[...]
     )
-    columns = send_ref.shape[0] * ROWS
     row = iota((ROWS, columns), 0)
     lane = iota((ROWS, columns), 1) - tp * ROWS
     extra = jnp.where((lane >= 0) & (lane < ROWS), -1.0, 0.0)
@@ -253,27 +249,36 @@
     message = jnp.concatenate(
         [jnp.where(tail, extra, normed[:, :columns]), normed[:, columns:]], axis=1
     ).astype(jnp.bfloat16)
-    for p in range(send_ref.shape[0]):
-        send_ref[p] = message
+    send_ref[...] = message
     attn_buf[...] = attention
     res_buf[...] = residual
     lanes = pl.ds(pl.multiple_of(seq * feature, feature), feature)
     mine = attn_buf[:, lanes]
     for r in range(requests):
         attn_ref[r] = mine[r * steps : (r + 1) * steps].astype(jnp.bfloat16)
-    own_ref[...] = res_buf[:, lanes]
+    rest = res_buf[:, lanes]
+    for r in range(requests):
+        own_ref[r] = rest[r * steps : (r + 1) * steps]
 
 
 def feed(
-    capacity, steps, used, slices, router_ref, gate_ref, up_ref, down_ref, tokens, out_ref
+    capacity, steps, used, slices, router_ref, gate_ref, up_ref, down_ref, near_ref, far_ref,
+    out_ref, tokens,
 ):
-    count = tokens.shape[0] // ROWS
+    half = near_ref.shape[0]
+    count = 2 * half
     width = gate_ref.shape[1]
     experts = router_ref.shape[0]
-    seq_size, _, _, feature = out_ref.shape
+    seq_size, _, requests, _, feature = out_ref.shape
     seq = lax.axis_index("seq")
     tp = lax.axis_index("tp")
     columns = count * ROWS
+    core = tp % 2
+    for d in range(half):
+        chip = (tp // 2) ^ d
+        for ref, which in ((near_ref, core), (far_ref, 1 - core)):
+            start = pl.multiple_of((2 * chip + which) * ROWS, ROWS)
+            tokens[pl.ds(start, ROWS), :] = ref[d]
     ids = jnp.zeros((8, columns), jnp.float32)
     for p in range(count):
         ids = ids + tokens[p * ROWS : (p + 1) * ROWS, :columns].astype(jnp.float32)[8:]
@@ -315,23 +320,46 @@
     inner = (jax.nn.gelu(gate) * upward).astype(jnp.bfloat16)
     produced = jnp.dot(inner, down_ref[...], preferred_element_type=jnp.float32)
     shared = (produced * share).astype(jnp.bfloat16)
-    term = lax.dot_general(select, shared, TN, preferred_element_type=jnp.float32).astype(
-        jnp.bfloat16
-    )
+    term = lax.dot_general(select, shared, TN, preferred_element_type=jnp.float32)
     for s in range(seq_size):
         for p in range(count):
-            out_ref[s, p] = term[p * ROWS : (p + 1) * ROWS, s * feature : (s + 1) * feature]
-
-
-def finish(own_ref, terms_ref, out_ref):
-    requests, steps, _ = out_ref.shape
-    total = own_ref[...]
-    mixture = terms_ref[0].astype(jnp.float32)
-    for i in range(1, terms_ref.shape[0]):
-        mixture = mixture + terms_ref[i].astype(jnp.float32)
-    total = total + mixture
-    for r in range(requests):
-        out_ref[r] = total[r * steps : (r + 1) * steps].astype(jnp.bfloat16)
+            for r in range(requests):
+                start = p * ROWS + r * steps
+                out_ref[s, p, r] = term[
+                    start : start + steps, s * feature : (s + 1) * feature
+                ].astype(jnp.bfloat16)
+
+
+def limit(mebibytes):
+    return pltpu.CompilerParams(vmem_limit_bytes=mebibytes * 1024 * 1024)
+
+
+def stage(count, *refs):
+    sources, copies, sems = refs[1 : 1 + count], refs[1 + count : 1 + 2 * count], refs[-1]
+    moves = [
+        pltpu.make_async_copy(source, copy, sems.at[i])
+        for i, (source, copy) in enumerate(zip(sources, copies))
+    ]
+    for move in moves:
+        move.start()
+    for move in moves:
+        move.wait()
+
+
+def staged(after, *arrays):
+    anywhere = pl.BlockSpec(memory_space=pl.ANY)
+    count = len(arrays)
+    size = sum(2 * x.size for x in arrays)
+    return pl.pallas_call(
+        functools.partial(stage, count),
+        out_shape=tuple(pltpu.VMEM(x.shape, x.dtype) for x in arrays),
+        in_specs=[anywhere] * (1 + count),
+        out_specs=(anywhere,) * count,
+        scratch_shapes=[pltpu.SemaphoreType.DMA((count,))],
+        compiler_params=limit(4),
+        cost_estimate=pl.CostEstimate(flops=0, bytes_accessed=2 * size, transcendentals=0),
+        name="stage",
+    )(after, *[pltpu.with_memory_space_constraint(x, pltpu.HBM) for x in arrays])
 
 
 def body(
@@ -363,13 +391,10 @@
     smem = pl.BlockSpec(memory_space=pltpu.SMEM)
     hbm = pl.BlockSpec(memory_space=pltpu.HBM)
 
-    def limit(mebibytes):
-        return pltpu.CompilerParams(vmem_limit_bytes=mebibytes * 1024 * 1024)
-
     small = pltpu.VMEM((requests, steps, width), jnp.bfloat16)
     part = pl.pallas_call(
         attend,
-        out_shape=jax.ShapeDtypeStruct((seq_size, ROWS, width + LANES), jnp.bfloat16),
+        out_shape=pltpu.VMEM((ROWS, width + LANES), jnp.bfloat16),
         in_specs=[hbm] * 6,
         out_specs=vmem,
         scratch_shapes=[
@@ -392,15 +417,20 @@
             for x in (lengths, new_query, new_key, new_value, key_cache, value_cache)
         ]
     )
-    parts = lax.all_to_all(part, "seq", 0, 0, tiled=True)
+
+    def swapped(x, axis, size, d):
+        return lax.ppermute(x, axis, [(i, i ^ d) for i in range(size)])
+
+    out_weight, gate_weight = staged(part, out_weight, gate_weight)
+    parts = [part] + [swapped(part, "seq", seq_size, d) for d in range(1, seq_size)]
     attn_out, own_residual, packed = pl.pallas_call(
-        project,
+        functools.partial(project, seq_size, tp_size * ROWS),
         out_shape=(
             jax.ShapeDtypeStruct((requests, steps, feature), jnp.bfloat16),
-            jax.ShapeDtypeStruct((ROWS, feature), jnp.float32),
-            jax.ShapeDtypeStruct((tp_size, ROWS, width), jnp.bfloat16),
+            jax.ShapeDtypeStruct((requests, steps, feature), jnp.float32),
+            jax.ShapeDtypeStruct((ROWS, width), jnp.bfloat16),
         ),
-        in_specs=[smem, vmem, vmem, vmem, vmem],
+        in_specs=[smem] + [vmem] * (3 + seq_size),
         out_specs=(vmem, vmem, vmem),
         scratch_shapes=[
             pltpu.VMEM((ROWS, width), jnp.float32),
@@ -408,26 +438,27 @@
         ],
         compiler_params=limit(8),
         name="project",
-    )(expert_ids.transpose(0, 2, 1), hidden_in, norm_gain.reshape(1, width), out_weight, parts)
-    tokens = lax.all_to_all(packed, "tp", 0, 0, tiled=True).reshape(tp_size * ROWS, width)
+    )(expert_ids.transpose(0, 2, 1), hidden_in, norm_gain.reshape(1, width), out_weight, *parts)
+    up_weight, down_weight = staged(packed, up_weight, down_weight)
+    near = jnp.stack(
+        [packed] + [swapped(packed, "tp", tp_size, 2 * d) for d in range(1, tp_size // 2)]
+    )
+    far = swapped(near, "tp", tp_size, 1)
     terms = pl.pallas_call(
         functools.partial(feed, capacity, steps, requests * steps, slices),
-        out_shape=jax.ShapeDtypeStruct((seq_size, tp_size, ROWS, feature), jnp.bfloat16),
-        in_specs=[vmem] * 5,
+        out_shape=jax.ShapeDtypeStruct(
+            (seq_size, tp_size, requests, steps, feature), jnp.bfloat16
+        ),
+        in_specs=[vmem] * 6,
         out_specs=vmem,
+        scratch_shapes=[pltpu.VMEM((tp_size * ROWS, width), jnp.bfloat16)],
         compiler_params=limit(16),
         name="feed",
-    )(router_weight.T, gate_weight, up_weight, down_weight, tokens)
-    terms = terms.reshape(seq_size * tp_size, ROWS, feature)
+    )(router_weight.T, gate_weight, up_weight, down_weight, near, far)
+    terms = terms.reshape(seq_size * tp_size, requests, steps, feature)
     arrived = lax.all_to_all(terms, ("seq", "tp"), 0, 0, tiled=True)
-    layer_out = pl.pallas_call(
-        finish,
-        out_shape=jax.ShapeDtypeStruct((requests, steps, feature), jnp.bfloat16),
-        in_specs=[vmem, vmem],
-        out_specs=vmem,
-        name="finish",
-    )(own_residual, arrived)
-    return (attn_out, layer_out)
+    mixture = jnp.sum(arrived.astype(jnp.float32), axis=0)
+    return (attn_out, (own_residual + mixture).astype(jnp.bfloat16))
 
 
 def solution(mesh):

time: 49.2 us -> 41.6 us (0.85); the launches traced: 48.3 us -> 42 us
  blocking collectives: 36.3 us -> 12.2 us
  starting transfers between devices: 0 us -> 11.5 us
  waiting for transfers between devices: 0 us -> 3.39 us
  Pallas kernels: 11.1 us -> 13.4 us
  other arithmetic: 0 us -> 0.72 us
    all_to_all x2 -> x0, blocking collectives: 22.7 us -> none  [the longest x1 14.9 us: body(): lax.all_to_all(packed, 'tp', 0, 0, tiled=True)]
    ppermute x0 -> x7, starting transfers between devices: none -> 11.5 us  [swapped(): return lax.ppermute(x, axis, [(i, i ^ d) for i in range(size)])]
    ppermute x0 -> x7, waiting for transfers between devices: none -> 3.39 us  [swapped(): return lax.ppermute(x, axis, [(i, i ^ d) for i in range(size)])]
    pallas_call x3 -> x4, Pallas kernels: 8.73 us -> 10.9 us  [the longest x2 5.17 us: staged(): pl.pallas_call(functools.partial(stage, count), out_shape=tuple((pltpu.VM...]
    all_to_all x1, blocking collectives: 13.7 us -> 12.2 us  [body(): arrived = lax.all_to_all(terms, ('seq', 'tp'), 0, 0, tiled=True)]
    convert_element_type x0 -> x1, other arithmetic: none -> 0.6 us  [body(): return (attn_out, (own_residual + mixture).astype(jnp.bfloat16))]
  transfers between devices with their start and end apart: 0 -> 7, of which waited for: 0 -> 2; matrix products, arithmetic and copies ran while one was open for 0% -> 0% of each run, Pallas kernels for 0% -> 12%
where the time goes in v3:
time: 41.6 us; the launch traced here: 42 us
  Pallas kernels  13.4 us (32%)
  blocking collectives  12.2 us (29%)
  starting transfers between devices  11.5 us (28%)
  waiting for transfers between devices  3.39 us (8%)
  between operations  0.78 us (2%)
  other arithmetic  0.72 us (2%)
    all_to_all x1, blocking collectives, body(): arrived = lax.all_to_all(terms, ('seq', 'tp'), 0, 0, tiled=True)  12.2 us
    ppermute x7, starting transfers between devices, swapped(): return lax.ppermute(x, axis, [(i, i ^ d) for i in range(size)])  11.5 us
    pallas_call x2, Pallas kernels, staged(): pl.pallas_call(functools.partial(stage, count), out_shape=tuple((pltpu.VM...  5.17 us
    pallas_call x1, Pallas kernels, body(): pl.pallas_call(attend, out_shape=pltpu.VMEM((ROWS, width + LANES), jnp.bf...  3.91 us
    ppermute x7, waiting for transfers between devices, swapped(): return lax.ppermute(x, axis, [(i, i ^ d) for i in range(size)])  3.39 us
    pallas_call x1, Pallas kernels, body(): pl.pallas_call(functools.partial(feed, capacity, steps, requests * steps,...  2.44 us
    pallas_call x1, Pallas kernels, body(): pl.pallas_call(functools.partial(project, seq_size, tp_size * ROWS), out_...  1.86 us
  transfers between devices with their start and end apart: 7, of which 2 were waited for; matrix products, arithmetic and copies ran while one was open for 0% of the time, Pallas kernels for 12%

profile of v3, /device:TPU:1, one launch (start us, length us, event | category | flops | bytes accessed | tf_op | source)
XLA Modules:
  0.0 42.0 jit_solution(2387773762826192243)
XLA Ops:
  0.6 3.9 %attend.1.refs_0_ = bf16[16,1152]{1,0:T(8,128)(2,1)S(1)} custom-call(s32[3]{0:T(128)} %lens_hbm.1, bf16[3,4,1024]{2,1,0:T(4,128)(2,1)} %q_hbm.1, bf16[3,4,1024]{2,1,0:T(4,128)(2,1)} %nk_hbm.1, bf16[3,4,1024]{2,1,0:T(4,128)(2,1)} %nv_hbm.1, bf16[3,1024,1024]{2,1,0:T(8,128)(2,1)} %k_hbm.1, bf16[3,1024,1024]{2,1,0:T(8,128)(2,1)} %v_hbm.1), custom_call_target="tpu_custom_call" | custom-call | tf_op jit(solution)/shard_map/attend/pallas_call | solution.py:395
  4.6 0.0 copy-start.1
  4.6 0.0 copy-start.2
  4.6 0.0 copy-start.3
  4.6 0.1 collective-permute-start.2
  4.7 0.2 collective-permute-start.1
  4.9 2.4 %collective-permute-start = (bf16[16,1152]{1,0:T(8,128)(2,1)S(1)}, bf16[16,1152]{1,0:T(8,128)(2,1)S(1)}, u32[]{:S(2)}, u32[]{:S(2)}) collective-permute-start(bf16[16,1152]{1,0:T(8,128)(2,1)S(1)} %attend.1.refs_0_), channel_id=1, source_target_pairs={{0,8},{8,0},{16,24},{24,16},{1,9},{9,1},{17,25},{25,17},{2,10},{10... | collective-permute-start | bytes 110600 | tf_op jit(solution)/shard_map/ppermute | solution.py:422
  7.3 2.5 %stage.2 = (bf16[1024,1024]{1,0:T(8,128)(2,1)S(1)}, bf16[1408,1024]{1,0:T(8,128)(2,1)S(1)}) custom-call(bf16[16,1152]{1,0:T(8,128)(2,1)S(1)} %attend.1.refs_0_, bf16[1024,1024]{1,0:T(8,128)(2,1)} %refs_1_.2, bf16[1408,1024]{1,0:T(8,128)(2,1)} %refs_2_.2), custom_call_target="tpu_custom_call" | custom-call | bytes 9961472 | tf_op jit(solution)/shard_map/stage/pallas_call | solution.py:353
  9.8 0.0 collective-permute-done.2.refs_3_
  9.8 0.0 collective-permute-done.1.refs_2_
  9.8 0.0 collective-permute-done.refs_1_
  9.8 0.0 copy-done.1
  9.8 0.0 copy-done.2
  9.8 0.0 copy-done.3
  9.8 1.9 %project.1 = (bf16[3,4,256]{2,1,0:T(4,128)(2,1)}, f32[3,4,256]{2,1,0:T(4,128)S(1)}, bf16[16,1024]{1,0:T(8,128)(2,1)S(1)}) custom-call(s32[3,2,4]{2,1,0:T(2,128)S(1)} %bitcast.12, bf16[3,4,1024]{2,1,0:T(4,128)(2,1)S(1)} %copy-done.1, f32[1,1024]{1,0:T(1,128)S(1)} %bitcast.11, bf16[1024,1024]{1,0:T(8,128)(2,1)S(1)} %get-tuple-element.9.weight_ref, ...), custom_call_target="tpu_custom_call" | custom-call | tf_op jit(solution)/shard_map/project/pallas_call | solution.py:426
  11.7 4.2 %collective-permute-start.5 = (bf16[16,1024]{1,0:T(8,128)(2,1)S(1)}, bf16[16,1024]{1,0:T(8,128)(2,1)S(1)}, u32[]{:S(2)}, u32[]{:S(2)}) collective-permute-start(bf16[16,1024]{1,0:T(8,128)(2,1)S(1)} %get-tuple-element.13.refs_0_), channel_id=1, source_target_pairs={{0,6},{1,7},{2,4},{3,5},{4,2},{5,3},{6,0},{7,1},{8,14},{9,15},{10,... | collective-permute-start | bytes 98312 | tf_op jit(solution)/shard_map/ppermute | solution.py:422
  15.8 0.0 collective-permute-start.4
  15.9 0.3 collective-permute-start.3
  16.1 1.0 %collective-permute-done.5 = bf16[16,1024]{1,0:T(8,128)(2,1)S(1)} collective-permute-done((bf16[16,1024]{1,0:T(8,128)(2,1)S(1)}, bf16[16,1024]{1,0:T(8,128)(2,1)S(1)}, u32[]{:S(2)}, u32[]{:S(2)}) %collective-permute-start.5) | collective-permute-done | bytes 32800 | tf_op jit(solution)/shard_map/ppermute | solution.py:422
  17.2 2.4 %collective-permute-done.4 = bf16[16,1024]{1,0:T(8,128)(2,1)S(1)} collective-permute-done((bf16[16,1024]{1,0:T(8,128)(2,1)S(1)}, bf16[16,1024]{1,0:T(8,128)(2,1)S(1)}, u32[]{:S(2)}, u32[]{:S(2)}) %collective-permute-start.4) | collective-permute-done | bytes 32800 | tf_op jit(solution)/shard_map/ppermute | solution.py:422
  19.5 0.0 collective-permute-done.3
  19.5 0.0 copy-start
  19.6 4.4 %collective-permute-start.6 = (bf16[4,16,1024]{2,1,0:T(8,128)(2,1)S(1)}, bf16[4,16,1024]{2,1,0:T(8,128)(2,1)S(1)}, u32[]{:S(2)}, u32[]{:S(2)}) collective-permute-start(bf16[4,16,1024]{2,1,0:T(8,128)(2,1)S(1)} %pad_maximum_fusion.near_ref), channel_id=1, source_target_pairs={{0,1},{1,0},{2,3},{3,2},{4,5},{5,4},{6,7},{7,6},{8,9},{9,8},{10,11... | collective-permute-start | bytes 393224 | tf_op jit(solution)/shard_map/ppermute | solution.py:422
  23.9 2.7 %stage.3 = (bf16[1408,1024]{1,0:T(8,128)(2,1)S(1)}, bf16[1408,1024]{1,0:T(8,128)(2,1)S(1)}) custom-call(bf16[16,1024]{1,0:T(8,128)(2,1)S(1)} %get-tuple-element.13.refs_0_, bf16[1408,1024]{1,0:T(8,128)(2,1)} %refs_1_.3, bf16[1408,1024]{1,0:T(8,128)(2,1)} %refs_2_.3), custom_call_target="tpu_custom_call" | custom-call | bytes 11534336 | tf_op jit(solution)/shard_map/stage/pallas_call | solution.py:353
  26.7 0.0 collective-permute-done.6.far_ref
  26.7 0.0 copy-done
  26.7 2.4 %feed.1 = bf16[4,8,3,4,256]{4,3,2,1,0:T(4,128)(2,1)S(1)} custom-call(bf16[16,1024]{1,0:T(8,128)(2,1)S(1)} %bitcast.10, bf16[1408,1024]{1,0:T(8,128)(2,1)S(1)} %get-tuple-element.12.gate_ref, bf16[1408,1024]{1,0:T(8,128)(2,1)S(1)} %get-tuple-element.14.up_ref, bf16[1408,1024]{1,0:T(8,128)(2,1)S(1)} %get-tuple-element.15.down_ref, ...), custom_call_target="tpu_custom_call" | custom-call | tf_op jit(solution)/shard_map/feed/pallas_call | solution.py:447
  29.1 12.2 %all_to_all.5 = bf16[32,3,4,256]{3,2,1,0:T(4,128)(2,1)S(1)} all-to-all(bf16[32,3,4,256]{3,2,1,0:T(4,128)(2,1)S(1)} %bitcast.8), channel_id=1, replica_groups=mesh['seq'=4,'tp'=8] {'seq','tp'}, dimensions={0} | all-to-all | bytes 393216 | tf_op jit(solution)/shard_map/all_to_all | solution.py:459
  41.3 0.1 convert_reduce_fusion
  41.4 0.6 %add_convert_fusion = bf16[3,4,256]{2,1,0:T(4,128)(2,1)} fusion(f32[3,4,256]{2,1,0:T(4,128)S(1)} %get-tuple-element.11, f32[3,4,256]{2,1,0:T(4,128)S(1)} %convert_reduce_fusion), kind=kLoop, calls=%fused_computation.2 | loop fusion | flops 6144 | bytes 30720 | tf_op jit(solution)/shard_map/convert_element_type | solution.py:461
  (1 shorter events, 0.0 us)
Async XLA Ops:
  4.6 5.3 %copy-start.1 = (bf16[3,4,1024]{2,1,0:T(4,128)(2,1)S(1)}, bf16[3,4,1024]{2,1,0:T(4,128)(2,1)}, u32[]{:S(2)}) copy-start(bf16[3,4,1024]{2,1,0:T(4,128)(2,1)} %hidden_ref.1) | copy-start | bytes 73732
  4.6 5.3 %copy-start.2 = (f32[1024]{0:T(1024)S(1)}, f32[1024]{0:T(1024)}, u32[]{:S(2)}) copy-start(f32[1024]{0:T(1024)} %param.22) | copy-start | bytes 12292
  4.6 5.3 %copy-start.3 = (s32[3,4,2]{1,2,0:T(2,128)S(1)}, s32[3,4,2]{1,2,0:T(2,128)}, u32[]{:S(2)}) copy-start(s32[3,4,2]{1,2,0:T(2,128)} %param.24) | copy-start | bytes 292
  4.6 5.2 %collective-permute-start.2 = (bf16[16,1152]{1,0:T(8,128)(2,1)S(1)}, bf16[16,1152]{1,0:T(8,128)(2,1)S(1)}, u32[]{:S(2)}, u32[]{:S(2)}) collective-permute-start(bf16[16,1152]{1,0:T(8,128)(2,1)S(1)} %attend.1.refs_0_), channel_id=1, source_target_pairs={{0,24},{8,16},{16,8},{24,0},{1,25},{9,17},{17,9},{25,1},{2,26},{10... | collective-permute-start | bytes 110600 | tf_op jit(solution)/shard_map/ppermute | solution.py:422
  4.7 5.1 %collective-permute-start.1 = (bf16[16,1152]{1,0:T(8,128)(2,1)S(1)}, bf16[16,1152]{1,0:T(8,128)(2,1)S(1)}, u32[]{:S(2)}, u32[]{:S(2)}) collective-permute-start(bf16[16,1152]{1,0:T(8,128)(2,1)S(1)} %attend.1.refs_0_), channel_id=1, source_target_pairs={{0,16},{8,24},{16,0},{24,8},{1,17},{9,25},{17,1},{25,9},{2,18},{10... | collective-permute-start | bytes 110600 | tf_op jit(solution)/shard_map/ppermute | solution.py:422
  4.9 4.9 %collective-permute-start = (bf16[16,1152]{1,0:T(8,128)(2,1)S(1)}, bf16[16,1152]{1,0:T(8,128)(2,1)S(1)}, u32[]{:S(2)}, u32[]{:S(2)}) collective-permute-start(bf16[16,1152]{1,0:T(8,128)(2,1)S(1)} %attend.1.refs_0_), channel_id=1, source_target_pairs={{0,8},{8,0},{16,24},{24,16},{1,9},{9,1},{17,25},{25,17},{2,10},{10... | collective-permute-start | bytes 110600 | tf_op jit(solution)/shard_map/ppermute | solution.py:422
  11.7 5.5 %collective-permute-start.5 = (bf16[16,1024]{1,0:T(8,128)(2,1)S(1)}, bf16[16,1024]{1,0:T(8,128)(2,1)S(1)}, u32[]{:S(2)}, u32[]{:S(2)}) collective-permute-start(bf16[16,1024]{1,0:T(8,128)(2,1)S(1)} %get-tuple-element.13.refs_0_), channel_id=1, source_target_pairs={{0,6},{1,7},{2,4},{3,5},{4,2},{5,3},{6,0},{7,1},{8,14},{9,15},{10,... | collective-permute-start | bytes 98312 | tf_op jit(solution)/shard_map/ppermute | solution.py:422
  15.8 3.7 %collective-permute-start.4 = (bf16[16,1024]{1,0:T(8,128)(2,1)S(1)}, bf16[16,1024]{1,0:T(8,128)(2,1)S(1)}, u32[]{:S(2)}, u32[]{:S(2)}) collective-permute-start(bf16[16,1024]{1,0:T(8,128)(2,1)S(1)} %get-tuple-element.13.refs_0_), channel_id=1, source_target_pairs={{0,4},{1,5},{2,6},{3,7},{4,0},{5,1},{6,2},{7,3},{8,12},{9,13},{10,... | collective-permute-start | bytes 98312 | tf_op jit(solution)/shard_map/ppermute | solution.py:422
  15.9 3.7 %collective-permute-start.3 = (bf16[16,1024]{1,0:T(8,128)(2,1)S(1)}, bf16[16,1024]{1,0:T(8,128)(2,1)S(1)}, u32[]{:S(2)}, u32[]{:S(2)}) collective-permute-start(bf16[16,1024]{1,0:T(8,128)(2,1)S(1)} %get-tuple-element.13.refs_0_), channel_id=1, source_target_pairs={{0,2},{1,3},{2,0},{3,1},{4,6},{5,7},{6,4},{7,5},{8,10},{9,11},{10,... | collective-permute-start | bytes 98312 | tf_op jit(solution)/shard_map/ppermute | solution.py:422
  19.5 7.1 %copy-start = (bf16[1024,16]{0,1:T(8,128)(2,1)S(1)}, bf16[1024,16]{0,1:T(8,128)(2,1)}, u32[]{:S(2)}) copy-start(bf16[1024,16]{0,1:T(8,128)(2,1)} %param.23) | copy-start | bytes 98308
  19.6 7.1 %collective-permute-start.6 = (bf16[4,16,1024]{2,1,0:T(8,128)(2,1)S(1)}, bf16[4,16,1024]{2,1,0:T(8,128)(2,1)S(1)}, u32[]{:S(2)}, u32[]{:S(2)}) collective-permute-start(bf16[4,16,1024]{2,1,0:T(8,128)(2,1)S(1)} %pad_maximum_fusion.near_ref), channel_id=1, source_target_pairs={{0,1},{1,0},{2,3},{3,2},{4,5},{5,4},{6,7},{7,6},{8,9},{9,8},{10,11... | collective-permute-start | bytes 393224 | tf_op jit(solution)/shard_map/ppermute | solution.py:422

commit v4 on v3

--- a/solution.py
+++ b/solution.py
@@ -11,6 +11,7 @@
 SHORT = 128
 ROWS = 16
 LANES = 128
+PIECES = 4
 masked_score = -1e30
 norm_epsilon = 1e-06
 NT = (((1,), (1,)), ((), ()))
@@ -33,7 +34,7 @@
 
 def attend(
     lens_hbm, q_hbm, nk_hbm, nv_hbm, k_hbm, v_hbm, out_ref,
-    lens, q_ref, nk_ref, nv_ref, kbuf, vbuf, acc, meta, sems, small_sems,
+    lens, q_ref, nk_ref, nv_ref, kbuf, vbuf, sems, small_sems,
 ):
     requests, block, width = k_hbm.shape
     steps = q_ref.shape[1]
@@ -64,20 +65,28 @@
         move.start()
     small[0].wait()
     left = [lens[r] - seq * block for r in range(requests)]
-    for r in range(requests):
-
-        @pl.when(left[r] >= block)
+    def begin(r, count, pieces):
+        size = count // pieces
+        for which, (src, dst) in enumerate(((k_hbm, kbuf), (v_hbm, vbuf))):
+            for i in range(pieces):
+                part = pl.ds(i * size, size)
+                pltpu.make_async_copy(
+                    src.at[r, part], dst.at[r, part], sems.at[which, r]
+                ).start()
+
+    full = [left[r] >= block for r in range(requests)]
+    short = [(left[r] > 0) & (left[r] < block) for r in range(requests)]
+    for r in range(requests):
+
+        @pl.when(short[r])
         def _():
-            for move in moves(r, block):
-                move.start()
-
-        @pl.when((left[r] > 0) & (left[r] < block))
+            begin(r, SHORT, 1)
+
+    for r in range(requests):
+
+        @pl.when(full[r])
         def _():
-            for move in moves(r, SHORT):
-                move.start()
-
-    acc[...] = jnp.zeros_like(acc)
-    meta[...] = jnp.where(iota(meta.shape, 1) // HEADS == 3, 1.0, 0.0)
+            begin(r, block, PIECES)
 
     for move in small[1:]:
         move.wait()
@@ -150,7 +159,7 @@
             spread.astype(jnp.bfloat16),
             preferred_element_type=jnp.float32,
         )
-        meta[r * steps : (r + 1) * steps, :] = gathered[:steps]
+        out_ref[r, :, width:] = gathered[:steps].astype(jnp.bfloat16)
         value_move.wait()
         for c in range(chunks):
             part_rows = slice(c * rows, (c + 1) * rows)
@@ -166,29 +175,28 @@
             half = mixed[: 2 * steps]
             for g in range(1, group // 2):
                 half = half + mixed[2 * steps * g : 2 * steps * (g + 1)]
-            acc[r * steps : (r + 1) * steps, lanes] = half[:steps] + half[steps:]
-
-    for r in range(requests):
-
-        @pl.when(left[r] >= block)
-        def _():
-            one(r, block, True)
-
-        @pl.when((left[r] > 0) & (left[r] < block))
-        def _():
-            one(r, SHORT, False)
+            out_ref[r, :, lanes] = (half[:steps] + half[steps:]).astype(jnp.bfloat16)
+
+    for r in range(requests):
 
         @pl.when(left[r] <= 0)
         def _():
             shape = (steps, LANES)
             hi, mid, low = three_parts(jnp.full(shape, masked_score, jnp.float32))
             part = iota(shape, 1) // HEADS
-            meta[r * steps : (r + 1) * steps, :] = jnp.where(
-                part == 0, hi, jnp.where(part == 1, mid, jnp.where(part == 2, low, 0.0))
-            )
-
-    out_ref[:, :width] = acc[...].astype(jnp.bfloat16)
-    out_ref[:, width:] = meta[...].astype(jnp.bfloat16)
+            empty = jnp.where(part == 0, hi, jnp.where(part == 1, mid, low))
+            out_ref[r, :, width:] = jnp.where(part < 3, empty, 0.0).astype(jnp.bfloat16)
+            out_ref[r, :, :width] = jnp.zeros((steps, width), jnp.bfloat16)
+
+        @pl.when(short[r])
+        def _():
+            one(r, SHORT, False)
+
+    for r in range(requests):
+
+        @pl.when(full[r])
+        def _():
+            one(r, block, True)
 
 
 def project(count, columns, ids_ref, hidden_ref, gain_ref, weight_ref, *refs):
@@ -203,15 +211,20 @@
     def moved(x, amount):
         return pltpu.roll(x, LANES - amount, 1)
 
+    def rows_of(ref, lanes):
+        pieces = [ref[r, :, lanes].astype(jnp.float32) for r in range(requests)]
+        blank = jnp.zeros((ROWS - requests * steps, pieces[0].shape[1]), jnp.float32)
+        return jnp.concatenate(pieces + [blank], axis=0)
+
     tops, totals = [], []
     for ref in parts:
-        x = ref[:, width:].astype(jnp.float32)
+        x = rows_of(ref, slice(width, width + LANES))
         tops.append(x + moved(x, HEADS) + moved(x, 2 * HEADS))
         totals.append(moved(x, 3 * HEADS) + moved(x, 4 * HEADS) + moved(x, 5 * HEADS))
     overall = functools.reduce(jnp.maximum, tops)
     factors = [jnp.exp(top - overall) for top in tops]
     total = functools.reduce(jnp.add, [f * t for f, t in zip(factors, totals)])
-    real = iota(total.shape, 1) < HEADS
+    real = (iota(total.shape, 1) < HEADS) & (iota(total.shape, 0) < requests * steps)
     inverse = jnp.where(real, 1.0 / jnp.where(real, total, 1.0), 0.0)
     ratio = jnp.concatenate([jnp.where(real, f, 0.0) * inverse for f in factors], axis=0)
     expand = jnp.where(
@@ -225,13 +238,11 @@
     wide = jnp.dot(packed.astype(jnp.bfloat16), expand, preferred_element_type=jnp.float32)
     context = jnp.zeros((ROWS, width), jnp.float32)
     for b, ref in enumerate(parts):
-        context = context + wide[b * ROWS : (b + 1) * ROWS] * ref[:, :width].astype(jnp.float32)
+        context = context + wide[b * ROWS : (b + 1) * ROWS] * rows_of(ref, slice(0, width))
     attention = jnp.dot(
         context.astype(jnp.bfloat16), weight_ref[...], preferred_element_type=jnp.float32
     )
-    hidden = [hidden_ref[r].astype(jnp.float32) for r in range(requests)]
-    hidden.append(jnp.zeros((ROWS - requests * steps, width), jnp.float32))
-    residual = jnp.concatenate(hidden, axis=0) + attention
+    residual = rows_of(hidden_ref, slice(0, width)) + attention
     normed = (
         residual
         * lax.rsqrt(jnp.mean(residual * residual, axis=1, keepdims=True) + norm_epsilon)
@@ -336,14 +347,14 @@
 
 def stage(count, *refs):
     sources, copies, sems = refs[1 : 1 + count], refs[1 + count : 1 + 2 * count], refs[-1]
-    moves = [
-        pltpu.make_async_copy(source, copy, sems.at[i])
-        for i, (source, copy) in enumerate(zip(sources, copies))
-    ]
-    for move in moves:
-        move.start()
-    for move in moves:
-        move.wait()
+    for i, (source, copy) in enumerate(zip(sources, copies)):
+        pieces = PIECES if source.shape[0] % (16 * PIECES) == 0 else 1
+        size = source.shape[0] // pieces
+        for piece in range(pieces):
+            part = pl.ds(piece * size, size)
+            pltpu.make_async_copy(source.at[part], copy.at[part], sems.at[i]).start()
+    for i, (source, copy) in enumerate(zip(sources, copies)):
+        pltpu.make_async_copy(source, copy, sems.at[i]).wait()
 
 
 def staged(after, *arrays):
@@ -394,7 +405,7 @@
     small = pltpu.VMEM((requests, steps, width), jnp.bfloat16)
     part = pl.pallas_call(
         attend,
-        out_shape=pltpu.VMEM((ROWS, width + LANES), jnp.bfloat16),
+        out_shape=pltpu.VMEM((requests, steps, width + LANES), jnp.bfloat16),
         in_specs=[hbm] * 6,
         out_specs=vmem,
         scratch_shapes=[
@@ -404,8 +415,6 @@
             small,
             pltpu.VMEM((requests, block, width), jnp.bfloat16),
             pltpu.VMEM((requests, block, width), jnp.bfloat16),
-            pltpu.VMEM((ROWS, width), jnp.float32),
-            pltpu.VMEM((ROWS, LANES), jnp.float32),
             pltpu.SemaphoreType.DMA((2, requests)),
             pltpu.SemaphoreType.DMA((4,)),
         ],
@@ -426,7 +435,7 @@
     attn_out, own_residual, packed = pl.pallas_call(
         functools.partial(project, seq_size, tp_size * ROWS),
         out_shape=(
-            jax.ShapeDtypeStruct((requests, steps, feature), jnp.bfloat16),
+            pltpu.VMEM((requests, steps, feature), jnp.bfloat16),
             jax.ShapeDtypeStruct((requests, steps, feature), jnp.float32),
             jax.ShapeDtypeStruct((ROWS, width), jnp.bfloat16),
         ),
@@ -443,6 +452,7 @@
     near = jnp.stack(
         [packed] + [swapped(packed, "tp", tp_size, 2 * d) for d in range(1, tp_size // 2)]
     )
+    near, up_weight, down_weight = lax.optimization_barrier((near, up_weight, down_weight))
     far = swapped(near, "tp", tp_size, 1)
     terms = pl.pallas_call(
         functools.partial(feed, capacity, steps, requests * steps, slices),

time: 41.6 us -> 42.3 us (1.017); the launches traced: 42 us -> 42.1 us
  blocking collectives: 12.2 us -> 0 us
  waiting for transfers between devices: 3.39 us -> 9.94 us
  starting transfers between devices: 11.5 us -> 15.8 us
  Pallas kernels: 13.4 us -> 14.2 us
  local copies, waits for them, and re-layouts: 0.03 us -> 0.62 us
    all_to_all x1 -> x0, blocking collectives: 12.2 us -> none  [body(): arrived = lax.all_to_all(terms, ('seq', 'tp'), 0, 0, tiled=True)]
    all_to_all x0 -> x1, waiting for transfers between devices: none -> 8.7 us  [body(): arrived = lax.all_to_all(terms, ('seq', 'tp'), 0, 0, tiled=True)]
    all_to_all x0 -> x1, starting transfers between devices: none -> 3.76 us  [body(): arrived = lax.all_to_all(terms, ('seq', 'tp'), 0, 0, tiled=True)]
    ppermute x7, waiting for transfers between devices: 3.39 us -> 1.24 us  [swapped(): return lax.ppermute(x, axis, [(i, i ^ d) for i in range(size)])]
    pallas_call x1, Pallas kernels: 3.91 us -> 4.65 us  [body(): pl.pallas_call(attend, out_shape=pltpu.VMEM((requests, steps, width + LAN...]
    pallas_call x1, Pallas kernels: 2.44 us -> 3.12 us  [body(): pl.pallas_call(functools.partial(feed, capacity, steps, requests * steps,...]
    unnamed x8 -> x9, local copies, waits for them, and re-layouts: 0.03 us -> 0.62 us
    ppermute x7, starting transfers between devices: 11.5 us -> 12.1 us  [swapped(): return lax.ppermute(x, axis, [(i, i ^ d) for i in range(size)])]
  transfers between devices with their start and end apart: 7 -> 8, of which waited for: 2 -> 4; matrix products, arithmetic and copies ran while one was open for 0% -> 1% of each run, Pallas kernels for 12% -> 12%
where the time goes in v4:
time: 42.3 us; the launch traced here: 42.1 us
  starting transfers between devices  15.8 us (37%)
  Pallas kernels  14.2 us (34%)
  waiting for transfers between devices  9.94 us (23%)
  between operations  0.77 us (2%)
  other arithmetic  0.72 us (2%)
  local copies, waits for them, and re-layouts  0.62 us (1%)
    ppermute x7, starting transfers between devices, swapped(): return lax.ppermute(x, axis, [(i, i ^ d) for i in range(size)])  12.1 us
    all_to_all x1, waiting for transfers between devices, body(): arrived = lax.all_to_all(terms, ('seq', 'tp'), 0, 0, tiled=True)  8.7 us
    pallas_call x2, Pallas kernels, staged(): pl.pallas_call(functools.partial(stage, count), out_shape=tuple((pltpu.VM...  5.05 us
    pallas_call x1, Pallas kernels, body(): pl.pallas_call(attend, out_shape=pltpu.VMEM((requests, steps, width + LAN...  4.65 us
    all_to_all x1, starting transfers between devices, body(): arrived = lax.all_to_all(terms, ('seq', 'tp'), 0, 0, tiled=True)  3.76 us
    pallas_call x1, Pallas kernels, body(): pl.pallas_call(functools.partial(feed, capacity, steps, requests * steps,...  3.12 us
    pallas_call x1, Pallas kernels, body(): pl.pallas_call(functools.partial(project, seq_size, tp_size * ROWS), out_...  1.35 us
    ppermute x7, waiting for transfers between devices, swapped(): return lax.ppermute(x, axis, [(i, i ^ d) for i in range(size)])  1.24 us
  transfers between devices with their start and end apart: 8, of which 4 were waited for; matrix products, arithmetic and copies ran while one was open for 1% of the time, Pallas kernels for 12%

profile of v4, /device:TPU:1, one launch (start us, length us, event | category | flops | bytes accessed | tf_op | source)
XLA Modules:
  0.0 42.1 jit_solution(10613473626991144695)
XLA Ops:
  0.6 4.6 %attend.1.refs_0_ = bf16[3,4,1152]{2,1,0:T(4,128)(2,1)S(1)} custom-call(s32[3]{0:T(128)} %lens_hbm.1, bf16[3,4,1024]{2,1,0:T(4,128)(2,1)} %q_hbm.1, bf16[3,4,1024]{2,1,0:T(4,128)(2,1)} %nk_hbm.1, bf16[3,4,1024]{2,1,0:T(4,128)(2,1)} %nv_hbm.1, bf16[3,1024,1024]{2,1,0:T(8,128)(2,1)} %k_hbm.1, bf16[3,1024,1024]{2,1,0:T(8,128)(2,1)} %v_hbm.1), custom_call_target="tpu_custom_call" | custom-call | tf_op jit(solution)/shard_map/attend/pallas_call | solution.py:406
  5.3 0.0 copy-start.1
  5.3 0.0 copy-start.2
  5.3 0.0 copy-start.3
  5.3 2.1 %collective-permute-start.2 = (bf16[3,4,1152]{2,1,0:T(4,128)(2,1)S(1)}, bf16[3,4,1152]{2,1,0:T(4,128)(2,1)S(1)}, u32[]{:S(2)}, u32[]{:S(2)}) collective-permute-start(bf16[3,4,1152]{2,1,0:T(4,128)(2,1)S(1)} %attend.1.refs_0_), channel_id=1, source_target_pairs={{0,24},{8,16},{16,8},{24,0},{1,25},{9,17},{17,9},{25,1},{2,26},{10... | collective-permute-start | bytes 82952 | tf_op jit(solution)/shard_map/ppermute | solution.py:431
  7.4 0.2 collective-permute-start.1
  7.6 0.4 collective-permute-start
  8.0 2.4 %stage.2 = (bf16[1024,1024]{1,0:T(8,128)(2,1)S(1)}, bf16[1408,1024]{1,0:T(8,128)(2,1)S(1)}) custom-call(bf16[3,4,1152]{2,1,0:T(4,128)(2,1)S(1)} %attend.1.refs_0_, bf16[1024,1024]{1,0:T(8,128)(2,1)} %refs_1_.2, bf16[1408,1024]{1,0:T(8,128)(2,1)} %refs_2_.2), custom_call_target="tpu_custom_call" | custom-call | bytes 9961472 | tf_op jit(solution)/shard_map/stage/pallas_call | solution.py:364
  10.5 0.0 collective-permute-done.2.refs_3_
  10.5 0.0 collective-permute-done.1.refs_2_
  10.5 0.0 collective-permute-done.refs_1_
  10.5 0.0 copy-done.1
  10.5 0.0 copy-done.2
  10.5 0.0 copy-done.3
  10.5 1.4 %project.1 = (bf16[3,4,256]{2,1,0:T(4,128)(2,1)S(1)}, f32[3,4,256]{2,1,0:T(4,128)S(1)}, bf16[16,1024]{1,0:T(8,128)(2,1)S(1)}) custom-call(s32[3,2,4]{2,1,0:T(2,128)S(1)} %bitcast.11, bf16[3,4,1024]{2,1,0:T(4,128)(2,1)S(1)} %copy-done.1, f32[1,1024]{1,0:T(1,128)S(1)} %bitcast.10, bf16[1024,1024]{1,0:T(8,128)(2,1)S(1)} %get-tuple-element.12.weight_ref, ...), custom_call_target="tpu_custom_call" | custom-call | tf_op jit(solution)/shard_map/project/pallas_call | solution.py:435
  11.9 0.0 copy-start
  11.9 3.5 %collective-permute-start.5 = (bf16[16,1024]{1,0:T(8,128)(2,1)S(1)}, bf16[16,1024]{1,0:T(8,128)(2,1)S(1)}, u32[]{:S(2)}, u32[]{:S(2)}) collective-permute-start(bf16[16,1024]{1,0:T(8,128)(2,1)S(1)} %get-tuple-element.16.refs_0_), channel_id=1, source_target_pairs={{0,6},{1,7},{2,4},{3,5},{4,2},{5,3},{6,0},{7,1},{8,14},{9,15},{10,... | collective-permute-start | bytes 98312 | tf_op jit(solution)/shard_map/ppermute | solution.py:431
  15.4 0.7 %collective-permute-start.4 = (bf16[16,1024]{1,0:T(8,128)(2,1)S(1)}, bf16[16,1024]{1,0:T(8,128)(2,1)S(1)}, u32[]{:S(2)}, u32[]{:S(2)}) collective-permute-start(bf16[16,1024]{1,0:T(8,128)(2,1)S(1)} %get-tuple-element.16.refs_0_), channel_id=1, source_target_pairs={{0,4},{1,5},{2,6},{3,7},{4,0},{5,1},{6,2},{7,3},{8,12},{9,13},{10,... | collective-permute-start | bytes 98312 | tf_op jit(solution)/shard_map/ppermute | solution.py:431
  16.1 0.2 collective-permute-start.3
  16.3 2.6 %stage.3 = (bf16[1408,1024]{1,0:T(8,128)(2,1)S(1)}, bf16[1408,1024]{1,0:T(8,128)(2,1)S(1)}) custom-call(bf16[16,1024]{1,0:T(8,128)(2,1)S(1)} %get-tuple-element.16.refs_0_, bf16[1408,1024]{1,0:T(8,128)(2,1)} %refs_1_.3, bf16[1408,1024]{1,0:T(8,128)(2,1)} %refs_2_.3), custom_call_target="tpu_custom_call" | custom-call | bytes 11534336 | tf_op jit(solution)/shard_map/stage/pallas_call | solution.py:364
  18.9 0.0 collective-permute-done.5
  19.0 0.2 collective-permute-done.4
  19.1 0.1 collective-permute-done.3
  19.2 5.0 %collective-permute-start.6 = (bf16[4,16,1024]{2,1,0:T(8,128)(2,1)S(1)}, bf16[4,16,1024]{2,1,0:T(8,128)(2,1)S(1)}, u32[]{:S(2)}, u32[]{:S(2)}) collective-permute-start(bf16[4,16,1024]{2,1,0:T(8,128)(2,1)S(1)} %pad_maximum_fusion.near_ref), channel_id=1, source_target_pairs={{0,1},{1,0},{2,3},{3,2},{4,5},{5,4},{6,7},{7,6},{8,9},{9,8},{10,11... | collective-permute-start | bytes 393224 | tf_op jit(solution)/shard_map/ppermute | solution.py:431
  24.2 1.0 %collective-permute-done.6.far_ref = bf16[4,16,1024]{2,1,0:T(8,128)(2,1)S(1)} collective-permute-done((bf16[4,16,1024]{2,1,0:T(8,128)(2,1)S(1)}, bf16[4,16,1024]{2,1,0:T(8,128)(2,1)S(1)}, u32[]{:S(2)}, u32[]{:S(2)}) %collective-permute-start.6) | collective-permute-done | bytes 131104 | tf_op jit(solution)/shard_map/ppermute | solution.py:431
  25.2 0.0 copy-done
  25.2 3.1 %feed.1 = bf16[4,8,3,4,256]{4,3,2,1,0:T(4,128)(2,1)} custom-call(bf16[16,1024]{1,0:T(8,128)(2,1)S(1)} %bitcast.9, bf16[1408,1024]{1,0:T(8,128)(2,1)S(1)} %get-tuple-element.15.gate_ref, bf16[1408,1024]{1,0:T(8,128)(2,1)S(1)} %get-tuple-element.19.up_ref, bf16[1408,1024]{1,0:T(8,128)(2,1)S(1)} %get-tuple-element.20.down_ref, ...), custom_call_target="tpu_custom_call" | custom-call | tf_op jit(solution)/shard_map/feed/pallas_call | solution.py:457
  28.3 3.8 %all-to-all-start = ((bf16[32,3,4,256]{3,2,1,0:T(4,128)(2,1)}), bf16[32,3,4,256]{3,2,1,0:T(4,128)(2,1)S(1)}, u32[]{:S(2)}, u32[]{:S(2)}) async-start(bf16[32,3,4,256]{3,2,1,0:T(4,128)(2,1)} %bitcast.7), calls=%async_computation | async-start | bytes 393216 | tf_op jit(solution)/shard_map/all_to_all | solution.py:469
  32.1 0.6 %copy.16 = bf16[3,4,256]{2,1,0:T(4,128)(2,1)} copy(bf16[3,4,256]{2,1,0:T(4,128)(2,1)S(1)} %get-tuple-element.22) | data formatting | bytes 12288
  32.7 8.7 %all-to-all-done = bf16[32,3,4,256]{3,2,1,0:T(4,128)(2,1)S(1)} async-done(((bf16[32,3,4,256]{3,2,1,0:T(4,128)(2,1)}), bf16[32,3,4,256]{3,2,1,0:T(4,128)(2,1)S(1)}, u32[]{:S(2)}, u32[]{:S(2)}) %all-to-all-start) | async-done | bytes 196640 | tf_op jit(solution)/shard_map/all_to_all | solution.py:469
  41.4 0.1 convert_reduce_fusion
  41.5 0.6 %add_convert_fusion = bf16[3,4,256]{2,1,0:T(4,128)(2,1)} fusion(f32[3,4,256]{2,1,0:T(4,128)S(1)} %get-tuple-element.14, f32[3,4,256]{2,1,0:T(4,128)S(1)} %convert_reduce_fusion), kind=kLoop, calls=%fused_computation.2 | loop fusion | flops 6144 | bytes 30720 | tf_op jit(solution)/shard_map/convert_element_type | solution.py:471
  (1 shorter events, 0.0 us)
Async XLA Ops:
  5.3 5.2 %copy-start.1 = (bf16[3,4,1024]{2,1,0:T(4,128)(2,1)S(1)}, bf16[3,4,1024]{2,1,0:T(4,128)(2,1)}, u32[]{:S(2)}) copy-start(bf16[3,4,1024]{2,1,0:T(4,128)(2,1)} %hidden_ref.1) | copy-start | bytes 73732
  5.3 5.2 %copy-start.2 = (f32[1024]{0:T(1024)S(1)}, f32[1024]{0:T(1024)}, u32[]{:S(2)}) copy-start(f32[1024]{0:T(1024)} %param.22) | copy-start | bytes 12292
  5.3 5.2 %copy-start.3 = (s32[3,4,2]{1,2,0:T(2,128)S(1)}, s32[3,4,2]{1,2,0:T(2,128)}, u32[]{:S(2)}) copy-start(s32[3,4,2]{1,2,0:T(2,128)} %param.24) | copy-start | bytes 292
  5.3 5.1 %collective-permute-start.2 = (bf16[3,4,1152]{2,1,0:T(4,128)(2,1)S(1)}, bf16[3,4,1152]{2,1,0:T(4,128)(2,1)S(1)}, u32[]{:S(2)}, u32[]{:S(2)}) collective-permute-start(bf16[3,4,1152]{2,1,0:T(4,128)(2,1)S(1)} %attend.1.refs_0_), channel_id=1, source_target_pairs={{0,24},{8,16},{16,8},{24,0},{1,25},{9,17},{17,9},{25,1},{2,26},{10... | collective-permute-start | bytes 82952 | tf_op jit(solution)/shard_map/ppermute | solution.py:431
  7.4 3.0 %collective-permute-start.1 = (bf16[3,4,1152]{2,1,0:T(4,128)(2,1)S(1)}, bf16[3,4,1152]{2,1,0:T(4,128)(2,1)S(1)}, u32[]{:S(2)}, u32[]{:S(2)}) collective-permute-start(bf16[3,4,1152]{2,1,0:T(4,128)(2,1)S(1)} %attend.1.refs_0_), channel_id=1, source_target_pairs={{0,16},{8,24},{16,0},{24,8},{1,17},{9,25},{17,1},{25,9},{2,18},{10... | collective-permute-start | bytes 82952 | tf_op jit(solution)/shard_map/ppermute | solution.py:431
  7.6 2.8 %collective-permute-start = (bf16[3,4,1152]{2,1,0:T(4,128)(2,1)S(1)}, bf16[3,4,1152]{2,1,0:T(4,128)(2,1)S(1)}, u32[]{:S(2)}, u32[]{:S(2)}) collective-permute-start(bf16[3,4,1152]{2,1,0:T(4,128)(2,1)S(1)} %attend.1.refs_0_), channel_id=1, source_target_pairs={{0,8},{8,0},{16,24},{24,16},{1,9},{9,1},{17,25},{25,17},{2,10},{10... | collective-permute-start | bytes 82952 | tf_op jit(solution)/shard_map/ppermute | solution.py:431
  11.9 13.3 %copy-start = (bf16[1024,16]{0,1:T(8,128)(2,1)S(1)}, bf16[1024,16]{0,1:T(8,128)(2,1)}, u32[]{:S(2)}) copy-start(bf16[1024,16]{0,1:T(8,128)(2,1)} %param.23) | copy-start | bytes 98308
  11.9 7.1 %collective-permute-start.5 = (bf16[16,1024]{1,0:T(8,128)(2,1)S(1)}, bf16[16,1024]{1,0:T(8,128)(2,1)S(1)}, u32[]{:S(2)}, u32[]{:S(2)}) collective-permute-start(bf16[16,1024]{1,0:T(8,128)(2,1)S(1)} %get-tuple-element.16.refs_0_), channel_id=1, source_target_pairs={{0,6},{1,7},{2,4},{3,5},{4,2},{5,3},{6,0},{7,1},{8,14},{9,15},{10,... | collective-permute-start | bytes 98312 | tf_op jit(solution)/shard_map/ppermute | solution.py:431
  15.4 3.8 %collective-permute-start.4 = (bf16[16,1024]{1,0:T(8,128)(2,1)S(1)}, bf16[16,1024]{1,0:T(8,128)(2,1)S(1)}, u32[]{:S(2)}, u32[]{:S(2)}) collective-permute-start(bf16[16,1024]{1,0:T(8,128)(2,1)S(1)} %get-tuple-element.16.refs_0_), channel_id=1, source_target_pairs={{0,4},{1,5},{2,6},{3,7},{4,0},{5,1},{6,2},{7,3},{8,12},{9,13},{10,... | collective-permute-start | bytes 98312 | tf_op jit(solution)/shard_map/ppermute | solution.py:431
  16.1 3.1 %collective-permute-start.3 = (bf16[16,1024]{1,0:T(8,128)(2,1)S(1)}, bf16[16,1024]{1,0:T(8,128)(2,1)S(1)}, u32[]{:S(2)}, u32[]{:S(2)}) collective-permute-start(bf16[16,1024]{1,0:T(8,128)(2,1)S(1)} %get-tuple-element.16.refs_0_), channel_id=1, source_target_pairs={{0,2},{1,3},{2,0},{3,1},{4,6},{5,7},{6,4},{7,5},{8,10},{9,11},{10,... | collective-permute-start | bytes 98312 | tf_op jit(solution)/shard_map/ppermute | solution.py:431
  19.2 6.0 %collective-permute-start.6 = (bf16[4,16,1024]{2,1,0:T(8,128)(2,1)S(1)}, bf16[4,16,1024]{2,1,0:T(8,128)(2,1)S(1)}, u32[]{:S(2)}, u32[]{:S(2)}) collective-permute-start(bf16[4,16,1024]{2,1,0:T(8,128)(2,1)S(1)} %pad_maximum_fusion.near_ref), channel_id=1, source_target_pairs={{0,1},{1,0},{2,3},{3,2},{4,5},{5,4},{6,7},{7,6},{8,9},{9,8},{10,11... | collective-permute-start | bytes 393224 | tf_op jit(solution)/shard_map/ppermute | solution.py:431
  28.3 13.1 %all-to-all-start = ((bf16[32,3,4,256]{3,2,1,0:T(4,128)(2,1)}), bf16[32,3,4,256]{3,2,1,0:T(4,128)(2,1)S(1)}, u32[]{:S(2)}, u32[]{:S(2)}) async-start(bf16[32,3,4,256]{3,2,1,0:T(4,128)(2,1)} %bitcast.7), calls=%async_computation | async-start | bytes 393216 | tf_op jit(solution)/shard_map/all_to_all | solution.py:469
